TPU v7x, 128 devices: a whole 4x4x4 slice. The times are simulated.
128 devices in a mesh: inst: 8 (over x_hi, z), tp: 16 (over x_lo, y, core).
Axes of the slice: x: 4 (x_hi: 2, x_lo: 2; x = x_hi * 2 + x_lo), y: 4, z: 4, core: 2. Of those that a mesh axis runs over, the one named last changes fastest.
Arguments:
- prompt: bfloat16 [8192, 4096], P('inst', 'tp'), may hold values from -6 to 6
- decode_tokens: bfloat16 [2, 128, 4096], P(None, 'inst', 'tp'), may hold values from -6 to 6
- query_weight: bfloat16 [4096, 4096], P(None, 'tp'), as said below
- key_weight: bfloat16 [4096, 4096], P(None, 'tp'), as said below
- value_weight: bfloat16 [4096, 4096], P(None, 'tp'), may hold values from -0.09375 to 0.09375
- out_weight: bfloat16 [4096, 4096], P('tp'), may hold values from -0.09375 to 0.09375
- cache_keys: bfloat16 [128, 32, 16, 4096], P(None, 'inst', None, 'tp'), may hold values from -6 to 6
- cache_values: bfloat16 [128, 32, 16, 4096], P(None, 'inst', None, 'tp'), may hold values from -6 to 6
- stretch_lengths: int32 [8], replicated, may hold values from 1 to 1024, 6144 in all
- panel_map: int32 [128, 32], P(None, 'inst'), may hold values from 0 to 31, each once within a row
- ctx_lengths: int32 [128], replicated, may hold values from 1 to 512, 32768 in all
Outputs:
- prefill_out: float32 [8192, 4096], P('inst', 'tp')
- decode_out: float32 [2, 128, 4096], P(None, 'inst', 'tp')
Inputs may be any that keep to these rules, and one draw needn't show every extreme that they name: `panel_map`: each row holds every panel number once. `query_weight`: scaled by the inverse square root of 4096. `key_weight`: scaled by the inverse square root of 4096.
All inputs are finite; a program needn't handle non-finite values.
Results may differ from a plain program's by a relative error of at most 0.01005.
Values may be sent and summed in bfloat16 or wider, within the bound.
No kernel may reach another device: no remote copies, remote signals or barrier semaphores. Data moves between devices by JAX's collectives and lax.ppermute only.
A program may use at most 128 MiB of HBM per device.

v0:
```python
import functools
import math

import jax
import jax.numpy as jnp
from jax import lax
from jax.experimental import pallas as pl
from jax.experimental.pallas import tpu as pltpu
from jax.sharding import PartitionSpec as P

HD = 128
CH = 1024
PANEL = 16
STEPS = 2
NEGATIVE = -1e30
SCALE = math.log2(math.e) / math.sqrt(HD)
AX = ("inst", "tp")
HALF = 512
GROUP = 256
DEC = 16
ROWS = HALF + DEC
CUT = 256
BF = jnp.bfloat16
F32 = jnp.float32
MIB = 1 << 20


def perm(dxh=0, dz=0, dxl=0, dy=0, dc=0, only_xh=None, zxor=0):
    pairs = []
    for xh in range(2):
        if only_xh is not None and xh != only_xh:
            continue
        for z in range(4):
            for xl in range(2):
                for y in range(4):
                    for c in range(2):
                        source = (xh * 4 + z) * 16 + xl * 8 + y * 2 + c
                        target = (
                            ((xh ^ dxh) * 4 + (((z + dz) % 4) ^ zxor)) * 16
                            + (xl ^ dxl) * 8
                            + ((y + dy) % 4) * 2
                            + (c ^ dc)
                        )
                        pairs.append((source, target))
    return pairs


def move(x, **steps):
    return lax.ppermute(x, AX, perm(**steps))


LOW = slice(0, CUT)
HIGH = ROWS - CUT


def gather_first(own):
    return own, move(own, dy=1), move(own, dy=-1), move(own, dxl=1)


def gather_second(first):
    _, before, after, beside = first
    up = move(jnp.concatenate([before[LOW], beside[CUT:]]), dy=1)
    down = move(jnp.concatenate([after[CUT:], beside[CUT:]]), dy=-1)
    across = move(jnp.concatenate([before[LOW], after[LOW]]), dxl=1)
    return up, down, across


def gather_third(second):
    _, down, across = second
    return move(across[LOW], dy=1), move(down[HIGH:], dy=-1)


STEPS_OF = (
    (
        ((0, 0), (0, -1), (0, 1), (1, 0)),
        tuple((n, 0, n, 0, ROWS) for n in range(4)),
    ),
    (
        ((0, 2), (1, -1), (1, 1)),
        (
            (0, 0, 0, 0, CUT), (0, CUT, 1, CUT, HIGH),
            (1, 0, 0, CUT, HIGH), (1, HIGH, 2, CUT, HIGH),
            (2, 0, 1, 0, CUT), (2, CUT, 2, 0, CUT),
        ),
    ),
    (((1, 2),), ((0, 0, 0, 0, CUT), (1, 0, 0, CUT, HIGH))),
)


def chip_at(idx, dx, dy):
    x = idx[2]
    x = 1 - x if dx else x
    return x * 4 + lax.rem(idx[3] + dy + 4, 4)


def qkv_kernel(step, idx, *refs):
    chips, parts = STEPS_OF[step]
    count = (4, 3, 2)[step]
    pieces, weights, refs = refs[:count], refs[count : count + 6], refs[count + 6 :]
    total, refs = (refs[0], refs[1:]) if step else (None, refs)
    xs, ws, sems = refs[-3:]
    core, z = idx[0], idx[1]
    copies = []
    for n in range(6):
        for place, (dx, dy) in enumerate(chips):
            rows = pl.ds(pl.multiple_of(chip_at(idx, dx, dy) * 512, 512), 512)
            copies.append(
                pltpu.make_async_copy(
                    weights[n].at[rows, :],
                    ws.at[n, pl.ds(place * 512, 512), :],
                    sems.at[len(copies)],
                )
            )
    for copy in copies:
        copy.start()
    for n, row, place, start, size in parts:
        for half in range(2):
            side = core if half == 0 else 1 - core
            column = pl.multiple_of(place * 512 + side * 256, 256)
            xs[start : start + size, pl.ds(column, 256)] = pieces[n][
                row : row + size, half * 256 : (half + 1) * 256
            ]

    def product(n):
        for place in range(len(chips)):
            pltpu.make_async_copy(
                weights[0].at[pl.ds(0, 512), :],
                ws.at[n, pl.ds(place * 512, 512), :],
                sems.at[n * len(chips) + place],
            ).wait()
        result = jnp.dot(xs[...], ws[n], preferred_element_type=F32)
        return result if total is None else result + total[n]

    if step < 2:

        def one(n, _):
            refs[0][n] = product(n)

        lax.fori_loop(0, 6, one, None)
        return
    for n in range(6):
        result = product(n)
        y_ref, z_refs = refs[0], refs[1:5]
        rel, kind = n // 3, n % 3
        owner = core if rel == 0 else 1 - core
        if kind == 0:
            result = result * SCALE
        result = result.astype(BF)
        for head in range(2):
            slot = lax.rem(owner * 2 + head - z + 4, 4)
            for k in range(4):

                @pl.when(slot == k)
                def _():
                    z_refs[k][:HALF, kind * 128 : (kind + 1) * 128] = result[
                        :HALF, head * 128 : (head + 1) * 128
                    ]

        if kind == 0:
            rows = slice(HALF + rel * DEC, HALF + (rel + 1) * DEC)
            for z_ref in z_refs:
                z_ref[rows, :256] = result[HALF:]
                z_ref[rows, 256:] = result[HALF:, :128]
        if rel == 1:
            refs[5][:, kind * 256 : (kind + 1) * 256] = result
        else:
            y_ref[:, kind * 256 : (kind + 1) * 256] = result


def vmem_spec():
    return pl.BlockSpec(memory_space=pltpu.VMEM)


def smem_spec():
    return pl.BlockSpec(memory_space=pltpu.SMEM)


def qkv(step, idx, pieces, weights, total=()):
    chips = len(STEPS_OF[step][0])
    shape = jax.ShapeDtypeStruct((6, ROWS, 256), F32)
    if step == 2:
        shape = (
            jax.ShapeDtypeStruct((ROWS, 768), BF),
            *[jax.ShapeDtypeStruct((HALF + 2 * DEC, 384), BF)] * 4,
            jax.ShapeDtypeStruct((ROWS, 768), BF),
        )
    return pl.pallas_call(
        functools.partial(qkv_kernel, step),
        out_shape=shape,
        in_specs=[smem_spec()]
        + [vmem_spec()] * len(pieces)
        + [pl.BlockSpec(memory_space=pltpu.HBM)] * 6
        + [vmem_spec()] * len(total),
        out_specs=(vmem_spec(),) * 6 if step == 2 else vmem_spec(),
        scratch_shapes=[
            pltpu.VMEM((ROWS, chips * 512), BF),
            pltpu.VMEM((6, chips * 512, 256), BF),
            pltpu.SemaphoreType.DMA((6 * chips,)),
        ],
        compiler_params=pltpu.CompilerParams(vmem_limit_bytes=(56, 40, 18)[step] * MIB),
        cost_estimate=pl.CostEstimate(
            flops=2 * ROWS * 512 * chips * 1536, bytes_accessed=8 * MIB, transcendentals=0
        ),
        name="qkv",
    )(idx, *pieces, *weights, *total)


def pack_kernel(a, b, c, d, out_ref):
    for n, piece in enumerate((a, b, c, d)):
        out_ref[n * HALF : (n + 1) * HALF, :] = piece[:HALF, 128:]


def pack(pieces):
    return pl.pallas_call(
        pack_kernel,
        out_shape=jax.ShapeDtypeStruct((4 * HALF, 256), BF),
        in_specs=[vmem_spec()] * 4,
        out_specs=vmem_spec(),
        compiler_params=pltpu.CompilerParams(vmem_limit_bytes=8 * MIB),
        cost_estimate=pl.CostEstimate(flops=0, bytes_accessed=4 * MIB, transcendentals=0),
        name="pack",
    )(*pieces)


def pack_weight_kernel(a, b, c, d, near_ref, far_ref):
    for n, piece in enumerate((a, b, c, d)):
        near_ref[n * 256 : (n + 1) * 256, :] = piece[:, :512]
        far_ref[n * 256 : (n + 1) * 256, :] = piece[:, 512:]


def pack_weight(pieces):
    return pl.pallas_call(
        pack_weight_kernel,
        out_shape=(jax.ShapeDtypeStruct((1024, 512), BF),) * 2,
        in_specs=[vmem_spec()] * 4,
        out_specs=(vmem_spec(),) * 2,
        compiler_params=pltpu.CompilerParams(vmem_limit_bytes=8 * MIB),
        cost_estimate=pl.CostEstimate(flops=0, bytes_accessed=4 * MIB, transcendentals=0),
        name="pack_weight",
    )(*pieces)


QT = 256
KT = 1024
PACKED = 5 * CH + 256


def wide(a, n):
    return jnp.concatenate([a] * n, axis=1)


def place_keys(idx, lens, base, mine, sib, ks, vs, offs):
    core, z = idx[0], idx[1]

    def block(b, offset):
        used = lens[base + b]
        row0 = pl.multiple_of(lax.rem(z - b + 4, 4) * HALF, HALF)
        offset = pl.multiple_of(offset, 16)
        offs[b] = offset
        first_mine = mine[pl.ds(row0, 16), :128].astype(F32)[:1]
        first_sib = sib[pl.ds(row0, 16), :128].astype(F32)[:1]
        filler = jnp.where(core == 0, first_mine, first_sib)
        for rel, source in enumerate((mine, sib)):
            side = core if rel == 0 else 1 - core
            for g in range(2):
                slot = g * 512 + side * 256
                rows = pl.ds(row0 + g * 256, 256)
                at = pl.ds(pl.multiple_of(offset + slot, 16), 256)

                @pl.when(slot + 256 <= used)
                def _():
                    ks[at, :] = source[rows, :128]
                    vs[at, :128] = source[rows, 128:]
                    vs[at, 128:] = jnp.ones((256, 128), BF)

                @pl.when((slot < used) & (slot + 256 > used))
                def _():
                    live = slot + lax.broadcasted_iota(jnp.int32, (256, 128), 0) < used
                    keys = source[rows, :128].astype(F32)
                    values = source[rows, 128:].astype(F32)
                    ks[at, :] = jnp.where(live, keys, filler).astype(BF)
                    vs[at, :128] = jnp.where(live, values, 0.0).astype(BF)
                    vs[at, 128:] = jnp.where(live, 1.0, 0.0).astype(BF)

        return offset + (used + 15) // 16 * 16

    end = lax.fori_loop(0, 4, block, 0)
    vs[pl.ds(pl.multiple_of(end, 16), KT), :] = jnp.zeros((KT, 256), BF)
    return end


def fold_tile(q, ks, vs, t, m_ref, acc_ref, i, limit_of):
    start = pl.multiple_of(t * KT, KT)
    keys = ks[pl.ds(start, KT), :]
    values = vs[pl.ds(start, KT), :]
    scores = [
        lax.dot_general(a, keys, (((1,), (1,)), ((), ())), preferred_element_type=F32) for a in q
    ]
    for g, s in enumerate(scores):
        if limit_of is not None:
            key = lax.broadcasted_iota(jnp.int32, (QT, KT), 1)
            s = jnp.where(key < limit_of(g) - start, s, NEGATIVE)
        rows = slice(g * QT, (g + 1) * QT)
        old = m_ref[i, rows]
        new = jnp.maximum(old, jnp.broadcast_to(jnp.max(s, axis=1, keepdims=True), (QT, 128)))
        p = jnp.exp2(s - wide(new, KT // 128)).astype(BF)
        acc_ref[i, rows] = acc_ref[i, rows] * wide(jnp.exp2(old - new), 2) + jnp.dot(
            p, values, preferred_element_type=F32
        )
        m_ref[i, rows] = new


def used_blocks(idx, lens, first, count, body):
    def one(i, _):
        block = lax.rem(idx[1] - first - i + 4, 4)
        used = lens[idx[4] * 4 + block]

        @pl.when(idx[0] * 256 < used)
        def _():
            body(i, block, used)

    lax.fori_loop(0, count, one, None)


def attend_own_kernel(idx, lens, q0, q1, q2, q3, mine, sib, acc_ref, m_ref, qs, ks, vs, offs):
    place_keys(idx, lens, idx[4] * 4, mine, sib, ks, vs, offs)
    for i, queries in enumerate((q0, q1, q2, q3)):
        qs[i] = queries[:HALF, :128]
    firsts = [g * 512 + idx[0] * 256 for g in range(2)]

    def body(i, block, used):
        offset = offs[block]
        q = [qs[i, g * QT : (g + 1) * QT, :] for g in range(2)]
        m_ref[i] = jnp.full((HALF, 128), NEGATIVE, F32)
        acc_ref[i] = jnp.zeros((HALF, 256), F32)

        def limit_of(g):
            return offset + firsts[g] + 1 + lax.broadcasted_iota(jnp.int32, (QT, KT), 0)

        limit = offset + jnp.minimum(firsts[1] + QT, used)
        whole = (offset + firsts[0] + 1) // KT
        tiles = (limit + KT - 1) // KT
        fold = functools.partial(fold_tile, q, ks, vs)
        lax.fori_loop(0, whole, lambda t, _: fold(t, m_ref, acc_ref, i, None), None)
        lax.fori_loop(whole, tiles, lambda t, _: fold(t, m_ref, acc_ref, i, limit_of), None)

    used_blocks(idx, lens, 0, 4, body)


def attend_own(idx, lens, pieces, mine, sib):
    return pl.pallas_call(
        attend_own_kernel,
        out_shape=(
            jax.ShapeDtypeStruct((4, HALF, 256), F32),
            jax.ShapeDtypeStruct((4, HALF, 128), F32),
        ),
        in_specs=[smem_spec()] * 2 + [vmem_spec()] * 6,
        out_specs=(vmem_spec(), vmem_spec()),
        scratch_shapes=[
            pltpu.VMEM((4, HALF, 128), BF),
            pltpu.VMEM((PACKED, 128), BF),
            pltpu.VMEM((PACKED, 256), BF),
            pltpu.SMEM((4,), jnp.int32),
        ],
        compiler_params=pltpu.CompilerParams(vmem_limit_bytes=24 * MIB),
        cost_estimate=pl.CostEstimate(
            flops=4 * CH * CH * 512, bytes_accessed=4 * MIB, transcendentals=4 * CH * CH
        ),
        name="attend_own",
    )(idx, lens, *pieces, mine, sib)


def attend_cross_kernel(which, idx, lens, *refs):
    count = len(which)
    pieces = refs[:count]
    mine, sib, acc_in, m_in, o_ref, qs, ks, vs, offs, m_ref, acc_ref = refs[count:]

    @pl.when(idx[4] == 1)
    def _():
        offs[4] = place_keys(idx, lens, 0, mine, sib, ks, vs, offs)

    o_ref[...] = jnp.zeros((count, HALF, 128), BF)
    for i, queries in enumerate(pieces):
        qs[i] = queries[:HALF, :128]

    def body(i, block, used):
        acc_ref[0] = acc_in[which[0] + i]

        @pl.when(idx[4] == 1)
        def _():
            end = offs[4]
            q = [qs[i, g * QT : (g + 1) * QT, :] for g in range(2)]
            m_ref[0] = m_in[which[0] + i]
            fold = functools.partial(fold_tile, q, ks, vs)
            whole = end // KT
            lax.fori_loop(0, whole, lambda t, _: fold(t, m_ref, acc_ref, 0, None), None)

            @pl.when(whole * KT < end)
            def _():
                fold(whole, m_ref, acc_ref, 0, lambda g: end)

        for g in range(2):
            rows = slice(g * QT, (g + 1) * QT)
            row = g * 512 + idx[0] * 256 + lax.broadcasted_iota(jnp.int32, (QT, 128), 0)
            out = acc_ref[0, rows, :128] / acc_ref[0, rows, 128:]
            o_ref[i, rows, :] = jnp.where(row < used, out, 0.0).astype(BF)

    used_blocks(idx, lens, which[0], count, body)


def attend_cross(which, idx, lens, pieces, mine, sib, state):
    return pl.pallas_call(
        functools.partial(attend_cross_kernel, which),
        out_shape=jax.ShapeDtypeStruct((len(which), HALF, 128), BF),
        in_specs=[smem_spec()] * 2 + [vmem_spec()] * (len(which) + 4),
        out_specs=vmem_spec(),
        scratch_shapes=[
            pltpu.VMEM((len(which), HALF, 128), BF),
            pltpu.VMEM((PACKED, 128), BF),
            pltpu.VMEM((PACKED, 256), BF),
            pltpu.SMEM((5,), jnp.int32),
            pltpu.VMEM((1, HALF, 128), F32),
            pltpu.VMEM((1, HALF, 256), F32),
        ],
        compiler_params=pltpu.CompilerParams(vmem_limit_bytes=24 * MIB),
        cost_estimate=pl.CostEstimate(
            flops=4 * CH * CH * 512, bytes_accessed=4 * MIB, transcendentals=4 * CH * CH
        ),
        name="attend_cross",
    )(idx, lens, *pieces, mine, sib, *state)


def decode_kernel(idx, lens, q_ref, keys, values, ok_ref, own, sib, out_ref, kc, vc, tops, sums, outs, sems):
    core, me = idx[0], idx[5]
    used = lens[me]

    def loads(n):
        home = (idx[4] ^ (n // 4)) * 4 + lax.rem(idx[1] - lax.rem(n, 4) + 4, 4)
        rows = pl.ds(pl.multiple_of(home * 16, 16), 16)
        return home, (
            pltpu.make_async_copy(keys.at[rows], kc.at[n], sems.at[2 * n]),
            pltpu.make_async_copy(values.at[rows], vc.at[n], sems.at[2 * n + 1]),
        )

    for n in range(8):
        for load in loads(n)[1]:
            load.start()
    nt = (((1,), (1,)), ((), ()))
    at = lax.broadcasted_iota(jnp.int32, (256, HALF), 1)
    slot = (at // 256) * 512 + at % 256
    ok_own = slot + core * 256 < used
    ok_sib = slot + (1 - core) * 256 < used
    for head in range(2):
        cols = slice(head * 128, (head + 1) * 128)
        kcols = slice(256 + head * 128, 256 + (head + 1) * 128)
        vcols = slice(512 + head * 128, 512 + (head + 1) * 128)
        q = q_ref[:, cols]
        s_o = lax.dot_general(q, own[:HALF, kcols], nt, preferred_element_type=F32)
        s_s = lax.dot_general(q, sib[:HALF, kcols], nt, preferred_element_type=F32)
        s_o = jnp.where(ok_own, s_o, NEGATIVE)
        s_s = jnp.where(ok_sib, s_s, NEGATIVE)
        top = jnp.maximum(
            jnp.max(s_o, axis=1, keepdims=True), jnp.max(s_s, axis=1, keepdims=True)
        )
        p_o = jnp.exp2(s_o - top)
        p_s = jnp.exp2(s_s - top)
        total = jnp.sum(p_o, axis=1, keepdims=True) + jnp.sum(p_s, axis=1, keepdims=True)
        out = jnp.dot(p_o.astype(BF), own[:HALF, vcols], preferred_element_type=F32) + jnp.dot(
            p_s.astype(BF), sib[:HALF, vcols], preferred_element_type=F32
        )
        tops[head] = jnp.broadcast_to(top, (256, 128))
        sums[head] = jnp.broadcast_to(total, (256, 128))
        outs[head] = out
    row = lax.broadcasted_iota(jnp.int32, (32, CH), 0)
    key = lax.broadcasted_iota(jnp.int32, (32, CH), 1)
    same = (row // 16) * 8 + row % 8 == key // 64
    lane = lax.broadcasted_iota(jnp.int32, (32, 128), 1)

    def group(n, _):
        home, copies = loads(n)
        for copy in copies:
            copy.wait()
        keys_c = kc[n].reshape(CH, 256)
        values_c = vc[n].reshape(CH, 256)
        ok = same & (ok_ref[pl.ds(home, 1), :] > 0)
        rows = pl.ds(pl.multiple_of(n * 32, 32), 32)
        stats = []
        for head in range(2):
            cols = slice(head * 128, (head + 1) * 128)
            top = tops[head, rows, :1]
            s = lax.dot_general(
                q_ref[rows, cols], keys_c[:, cols], nt, preferred_element_type=F32
            )
            s = jnp.where(ok, s, NEGATIVE)
            new = jnp.maximum(top, jnp.max(s, axis=1, keepdims=True))
            p = jnp.exp2(s - new)
            factor = jnp.exp2(top - new)
            stats += [new, factor * sums[head, rows, :1] + jnp.sum(p, axis=1, keepdims=True)]
            out_ref[n, :, cols] = factor * outs[head, rows, :] + jnp.dot(
                p.astype(BF), values_c[:, cols], preferred_element_type=F32
            )
        out_ref[n, :, 256:] = jnp.where(
            lane < 32,
            stats[0],
            jnp.where(lane < 64, stats[1], jnp.where(lane < 96, stats[2], stats[3])),
        )

    lax.fori_loop(0, 8, group, None)


def decode_parts(idx, lens, queries, cache_keys, cache_values, ok, own, sib):
    hbm = pl.BlockSpec(memory_space=pltpu.HBM)
    return pl.pallas_call(
        decode_kernel,
        out_shape=jax.ShapeDtypeStruct((8, 32, 384), F32),
        in_specs=[smem_spec()] * 2 + [vmem_spec(), hbm, hbm] + [vmem_spec()] * 3,
        out_specs=vmem_spec(),
        scratch_shapes=[
            pltpu.VMEM((8, 16, 4, PANEL, 256), BF),
            pltpu.VMEM((8, 16, 4, PANEL, 256), BF),
            *[pltpu.VMEM((2, 256, 128), F32)] * 3,
            pltpu.SemaphoreType.DMA((16,)),
        ],
        compiler_params=pltpu.CompilerParams(vmem_limit_bytes=50 * MIB),
        cost_estimate=pl.CostEstimate(
            flops=8 * 32 * 2048 * 1024, bytes_accessed=10 * MIB, transcendentals=8 * 64 * 2048
        ),
        name="decode_parts",
    )(idx, lens, queries, cache_keys, cache_values, ok, own, sib)


def merge_kernel(parts, qkv_rows, out_ref):
    for head in range(2):
        cols = slice(head * 128, (head + 1) * 128)
        tops = [parts[n, :, 256 + head * 64 : 256 + head * 64 + 1] for n in range(8)]
        sums = [parts[n, :, 288 + head * 64 : 288 + head * 64 + 1] for n in range(8)]
        for side in range(2):
            for s in range(2):
                rows = slice(side * 16 + s * 8, side * 16 + s * 8 + 8)
                q = qkv_rows[rows, cols].astype(F32)
                fresh = []
                for u in range(s + 1):
                    from_rows = slice(side * 16 + u * 8, side * 16 + u * 8 + 8)
                    k = qkv_rows[from_rows, 256 + head * 128 : 384 + head * 128].astype(F32)
                    v = qkv_rows[from_rows, 512 + head * 128 : 640 + head * 128].astype(F32)
                    fresh.append((jnp.sum(q * k, axis=1, keepdims=True), v))
                top = fresh[0][0]
                for score, _ in fresh[1:]:
                    top = jnp.maximum(top, score)
                for part in tops:
                    top = jnp.maximum(top, part[rows])
                total = jnp.zeros((8, 1), F32)
                out = jnp.zeros((8, 128), F32)
                for score, v in fresh:
                    w = jnp.exp2(score - top)
                    total += w
                    out += w.astype(BF).astype(F32) * v
                for n in range(8):
                    w = jnp.exp2(tops[n][rows] - top)
                    total += w * sums[n][rows]
                    out += w * parts[n, rows, cols]
                out_ref[rows, cols] = (out / total).astype(BF)


def merge_parts(parts, qkv_rows):
    return pl.pallas_call(
        merge_kernel,
        out_shape=jax.ShapeDtypeStruct((32, 256), BF),
        in_specs=[vmem_spec()] * 2,
        out_specs=vmem_spec(),
        compiler_params=pltpu.CompilerParams(vmem_limit_bytes=4 * MIB),
        cost_estimate=pl.CostEstimate(flops=MIB, bytes_accessed=MIB, transcendentals=1000),
        name="merge_parts",
    )(parts, qkv_rows)


def head_order_kernel(idx, a, b, c, d, near, far, out_ref):
    for k, piece in enumerate((a, b, c, d)):
        column = pl.multiple_of(lax.rem(idx[1] + k - 2 * idx[0] + 4, 4) * 128, 128)
        out_ref[:HALF, pl.ds(column, 128)] = piece[...]
    out_ref[HALF:, :256] = near[...]
    out_ref[HALF:, 256:] = far[...]


def head_order(idx, pieces, near, far):
    return pl.pallas_call(
        head_order_kernel,
        out_shape=jax.ShapeDtypeStruct((ROWS, 512), BF),
        in_specs=[smem_spec()] + [vmem_spec()] * 6,
        out_specs=vmem_spec(),
        compiler_params=pltpu.CompilerParams(vmem_limit_bytes=4 * MIB),
        cost_estimate=pl.CostEstimate(flops=0, bytes_accessed=MIB, transcendentals=0),
        name="head_order",
    )(idx, *pieces, near, far)


def out_kernel(step, idx, *refs):
    chips, parts = STEPS_OF[step]
    count = (4, 3, 2)[step]
    pieces, ws, refs = refs[:count], refs[count : count + 4], refs[count + 4 :]
    totals, refs = (refs[:2], refs[2:]) if step else (None, refs)
    results, xs = refs[:2], refs[2]
    for n, row, place, start, size in parts:
        xs[start : start + size, place * 512 : (place + 1) * 512] = pieces[n][row : row + size, :]
    for rel in range(2):
        side = idx[0] if rel == 0 else 1 - idx[0]
        columns = pl.ds(pl.multiple_of(side * 256, 256), 256)
        result = None if totals is None else totals[rel][...]
        for place, (dx, dy) in enumerate(chips):
            k = -dy % 4
            for half, w in enumerate(ws[2 * dx : 2 * dx + 2]):
                at = place * 512 + half * 256
                term = jnp.dot(
                    xs[:, at : at + 256],
                    w[k * 256 : (k + 1) * 256, columns],
                    preferred_element_type=F32,
                )
                result = term if result is None else result + term
        results[rel][...] = result


def out_project(step, idx, pieces, weights, totals=()):
    chips = len(STEPS_OF[step][0])
    return pl.pallas_call(
        functools.partial(out_kernel, step),
        out_shape=(
            jax.ShapeDtypeStruct((ROWS, 256), F32),
            jax.ShapeDtypeStruct((ROWS, 256), F32),
        ),
        in_specs=[smem_spec()] + [vmem_spec()] * (len(pieces) + 4 + len(totals)),
        out_specs=(vmem_spec(), vmem_spec()),
        scratch_shapes=[pltpu.VMEM((ROWS, chips * 512), BF)],
        compiler_params=pltpu.CompilerParams(vmem_limit_bytes=20 * MIB),
        cost_estimate=pl.CostEstimate(
            flops=2 * ROWS * 512 * chips * 512, bytes_accessed=4 * MIB, transcendentals=0
        ),
        name="out_project",
    )(idx, *pieces, *weights, *totals)


def pick(pair, core):
    return jnp.where(core == 0, pair[0], pair[1])


def shards(
    prompt,
    decode_tokens,
    query_weight,
    key_weight,
    value_weight,
    out_weight,
    cache_keys,
    cache_values,
    stretch_lengths,
    panel_map,
    ctx_lengths,
):
    inst = lax.axis_index("inst")
    tp = lax.axis_index("tp")
    core = tp % 2
    y = (tp // 2) % 4
    x = tp // 8
    z = inst % 4
    xh = inst // 4
    idx = jnp.stack([core, z, x, y, xh, inst, 0, 0]).astype(jnp.int32)

    groups = prompt.reshape(2, 2, GROUP, 256)
    tokens = decode_tokens.reshape(STEPS, 2, 8, 256)
    halves = [
        jnp.concatenate(
            [groups[:, n].reshape(HALF, 256), tokens[:, n].reshape(DEC, 256)], axis=0
        )
        for n in range(2)
    ]
    mine, theirs = pick(halves, core), pick(halves[::-1], core)
    received = move(theirs, dc=1)
    query_w, key_w, received = lax.optimization_barrier((query_weight, key_weight, received))
    first = gather_first(jnp.concatenate([mine, received], axis=1))
    sib_query, sib_key = move(query_w, dc=1), move(key_w, dc=1)
    value_w, *rest = lax.optimization_barrier((value_weight, *first[1:]))
    first = (first[0], *rest)
    sib_value = move(value_w, dc=1)
    second = gather_second(first)
    weights = (query_weight, key_weight, value_weight, sib_query, sib_key, sib_value)
    total = qkv(0, idx, first, weights)
    total, *second = lax.optimization_barrier((total, *second))
    third = gather_third(second)
    total = qkv(1, idx, second, weights, (total,))
    own_rows, *by_head, rows_out = qkv(2, idx, third, weights, (total,))

    heads = [move(by_head[k], dz=k) for k in (1, 3, 2)]
    one, three, two, own = lax.optimization_barrier((*heads, by_head[0]))
    blocks = (own, one, two, three)
    mine = pack(blocks)
    cross = move(mine, dxh=1, only_xh=0)
    queries = jnp.stack([a[HALF:, :256].reshape(2, DEC, 256) for a in blocks])
    other_queries = move(queries, dxh=1)
    sib = move(mine, dc=1)

    rows_out, queries, other_queries, out_w = lax.optimization_barrier(
        (rows_out, queries, other_queries, out_weight)
    )
    queries = jnp.concatenate([queries, other_queries], axis=0)
    pair = (queries[:, 0], move(queries[:, 1], dc=1))
    from_sib = move(rows_out, dc=1)
    queries = jnp.concatenate([pick(pair, core), pick(pair[::-1], core)], axis=1)
    queries = queries.reshape(256, 256)
    pair = (own_rows[HALF:], from_sib[HALF:])
    dec_rows = jnp.concatenate([pick(pair, core), pick(pair[::-1], core)], axis=0)

    spread = []
    for dy in range(4):
        at = (y + dy) % 4 * 512
        columns = jnp.concatenate(
            [
                lax.dynamic_slice_in_dim(out_w, side * 2048 + at, 512, axis=1)
                for side in (x, 1 - x)
            ],
            axis=1,
        )
        spread.append(columns if dy == 0 else move(columns, dy=dy))

    positions = (
        panel_map[:, :, None] * PANEL + jnp.arange(PANEL, dtype=jnp.int32)[None, None, :]
    )
    ok = (positions < ctx_lengths[:, None, None]).astype(F32).reshape(8, CH)
    parts = decode_parts(
        idx, stretch_lengths, queries, cache_keys, cache_values, ok, own_rows, from_sib
    )
    moved = move(parts[4:], dxh=1)
    parts, mine = lax.optimization_barrier((parts, mine))
    state = attend_own(idx, stretch_lengths, blocks, mine, sib)
    *state, moved, cross = lax.optimization_barrier((*state, moved, cross))
    cross_sib = move(cross, dc=1)
    parts = jnp.stack([parts[:4], moved])
    moved = [move(parts[:, k], dz=4 - k) for k in (1, 2, 3)]
    near, far = pack_weight(spread)
    cross_sib, near, far = lax.optimization_barrier((cross_sib, near, far))
    far = move(far, dxl=1)
    first_heads = attend_cross(
        (1, 2, 3), idx, stretch_lengths, blocks[1:], cross, cross_sib, state
    )
    first_heads, *moved = lax.optimization_barrier((first_heads, *moved))
    back_one = move(first_heads[0], dz=3)
    back_two = move(first_heads[1], dz=2)
    back_three = move(first_heads[2], dz=1)
    parts = jnp.stack([parts[:, 0], *moved], axis=1).reshape(8, 32, 384)
    dec_attn = merge_parts(parts, dec_rows)
    theirs = move(pick((dec_attn[DEC:], dec_attn[:DEC]), core), dc=1)
    dec_attn, cross = lax.optimization_barrier((dec_attn, cross))
    mine = pick((dec_attn[:DEC], dec_attn[DEC:]), core)
    last_heads = attend_cross((0,), idx, stretch_lengths, (own,), cross, cross_sib, state)
    near, last_heads = lax.optimization_barrier((near, last_heads))
    attn = head_order(idx, (last_heads[0], back_one, back_two, back_three), mine, theirs)
    first = gather_first(attn)
    attn, near = lax.optimization_barrier((attn, near))
    weights = (near, move(near, dc=1), far, move(far, dc=1))
    second = gather_second(first)
    totals = out_project(0, idx, first, weights)
    *totals, up, down, across = lax.optimization_barrier((*totals, *second))
    second = (up, down, across)
    third = gather_third(second)
    totals = out_project(1, idx, second, weights, totals)
    mine, theirs = out_project(2, idx, third, weights, totals)
    received = move(theirs, dc=1)
    pair = (mine, received)
    sides = [pick(pair, core), pick(pair[::-1], core)]
    prefill_out = jnp.stack(
        [side[:HALF].reshape(2, GROUP, 256) for side in sides], axis=1
    ).reshape(CH, 256)
    decode_out = jnp.stack(
        [side[HALF:].reshape(STEPS, 8, 256) for side in sides], axis=1
    ).reshape(STEPS, 16, 256)
    return prefill_out, decode_out


def solution(mesh):
    return jax.shard_map(
        shards,
        mesh=mesh,
        in_specs=(
            P("inst", "tp"),
            P(None, "inst", "tp"),
            P(None, "tp"),
            P(None, "tp"),
            P(None, "tp"),
            P("tp", None),
            P(None, "inst", None, "tp"),
            P(None, "inst", None, "tp"),
            P(),
            P(None, "inst"),
            P(),
        ),
        out_specs=(P("inst", "tp"), P(None, "inst", "tp")),
        check_vma=False,
    )
```

profile of v0, /device:TPU:5, one launch (start us, length us, event | category | flops | bytes accessed | tf_op | source)
XLA Modules:
  0.0 201.4 jit_solution(17595035701688367073)
XLA Ops:
  0.6 1.1 fusion.8
  1.7 0.9 slice_bitcast_fusion.9
  2.7 0.8 collective-permute-start
  3.5 1.2 collective-permute-done
  4.7 1.4 collective-permute-start.1
  6.1 1.5 collective-permute-start.2
  7.6 0.9 collective-permute-start.3
  8.5 1.1 collective-permute-start.4
  9.6 10.0 %collective-permute-done.1.refs_1_ = bf16[528,512]{1,0:T(8,128)(2,1)S(1)} collective-permute-done((bf16[528,512]{1,0:T(8,128)(2,1)S(1)}, bf16[528,512]{1,0:T(8,128)(2,1)S(1)}, u32[]{:S(2)}, u32[]{:S(2)}) %collective-permute-start.1) | collective-permute-done | bytes 540704 | tf_op jit(solution)/shard_map/ppermute | solution.py:49
  19.6 1.0 collective-permute-done.3.refs_3_
  20.6 1.7 collective-permute-start.6
  22.3 0.8 pad_maximum_fusion.1
  23.2 1.4 collective-permute-start.8
  24.6 0.9 pad_maximum_fusion.4
  25.6 0.9 pad_maximum_fusion.6
  26.5 1.3 copy-done.4
  27.8 0.9 collective-permute-start.9
  29.4 10.1 %qkv.3.refs_9_ = f32[6,528,256]{2,1,0:T(8,128)} custom-call(s32[8]{0:T(128)} %stack.57.idx, bf16[528,512]{1,0:T(8,128)(2,1)} %copy-done.11, bf16[528,512]{1,0:T(8,128)(2,1)} %copy-done.15, bf16[528,512]{1,0:T(8,128)(2,1)} %copy-done.12, bf16[528,512]{1,0:T(8,128)(2,1)} %copy-done.14, bf16[4096,256]{1,0:T(8,128)(2,1)} %refs_2_.1, bf16[4096,256]{1,0:T(8,128)(2,1)} %refs_3_.3, ...), custom_call_target="tpu_custom_call" | custom-call | flops 3321888768 | bytes 8388608 | tf_op jit(solution)/shard_map/qkv/pallas_call | solution.py:187
  40.1 2.6 %collective-permute-start.11 = (bf16[272,512]{1,0:T(8,128)(2,1)S(1)}, bf16[272,512]{1,0:T(8,128)(2,1)S(1)}, u32[]{:S(2)}, u32[]{:S(2)}) collective-permute-start(bf16[272,512]{1,0:T(8,128)(2,1)S(1)} %slice.136), channel_id=1, source_target_pairs={{0,6},{1,7},{2,0},{3,1},{4,2},{5,3},{6,4},{7,5},{8,14},{9,15},{10,... | collective-permute-start | bytes 835592 | tf_op jit(solution)/shard_map/ppermute | solution.py:49
  42.9 1.6 copy-done.5
  44.5 7.7 %qkv.4.refs_8_ = f32[6,528,256]{2,1,0:T(8,128)} custom-call(s32[8]{0:T(128)S(1)} %copy-done.7, bf16[528,512]{1,0:T(8,128)(2,1)S(1)} %collective-permute-done.7.refs_0_, bf16[544,512]{1,0:T(8,128)(2,1)S(1)} %collective-permute-done.8.refs_1_, bf16[512,512]{1,0:T(8,128)(2,1)S(1)} %collective-permute-done.9.refs_2_, bf16[4096,256]{1,0:T(8,128)(2,1)S(1)} %copy-done.1, ...), custom_call_target="tpu_custom_call" | custom-call | flops 2491416576 | bytes 8388608 | tf_op jit(solution)/shard_map/qkv/pallas_call | solution.py:187
  52.2 1.9 copy-done.6
  54.1 4.8 %qkv.5 = (bf16[528,768]{1,0:T(8,128)(2,1)S(1)}, bf16[544,384]{1,0:T(8,128)(2,1)S(1)}, bf16[544,384]{1,0:T(8,128)(2,1)}, bf16[544,384]{1,0:T(8,128)(2,1)S(1)}, bf...) custom-call(s32[8]{0:T(128)S(1)} %copy-done.7, bf16[256,512]{1,0:T(8,128)(2,1)S(1)} %collective-permute-done.10.refs_0_, ...), custom_call_target="tpu_custom_call" | custom-call | flops 830472192 | bytes 8388608 | tf_op jit(solution)/shard_map/qkv/pallas_call | solution.py:187
  58.9 0.9 copy-done.9
  59.8 1.6 collective-permute-start.12
  61.4 2.1 %collective-permute-start.13 = (bf16[544,384]{1,0:T(8,128)(2,1)}, bf16[544,384]{1,0:T(8,128)(2,1)S(1)}, u32[]{:S(2)}, u32[]{:S(2)}) collective-permute-start(bf16[544,384]{1,0:T(8,128)(2,1)} %get-tuple-element.72), channel_id=1, source_target_pairs={{0,48},{1,49},{2,50},{3,51},{4,52},{5,53},{6,54},{7,55},{8,56},{9,... | collective-permute-start | bytes 1253384 | tf_op jit(solution)/shard_map/ppermute | solution.py:49
  63.6 1.3 collective-permute-start.14
  65.0 6.2 %collective-permute-done.12.b.q1.refs_0_ = bf16[544,384]{1,0:T(8,128)(2,1)S(1)} collective-permute-done((bf16[544,384]{1,0:T(8,128)(2,1)}, bf16[544,384]{1,0:T(8,128)(2,1)S(1)}, u32[]{:S(2)}, u32[]{:S(2)}) %collective-permute-start.12) | collective-permute-done | bytes 417824 | tf_op jit(solution)/shard_map/ppermute | solution.py:49
  71.1 9.8 %collective-permute-done.14.c.q2.refs_1_ = bf16[544,384]{1,0:T(8,128)(2,1)S(1)} collective-permute-done((bf16[544,384]{1,0:T(8,128)(2,1)S(1)}, bf16[544,384]{1,0:T(8,128)(2,1)S(1)}, u32[]{:S(2)}, u32[]{:S(2)}) %collective-permute-start.14) | collective-permute-done | bytes 417824 | tf_op jit(solution)/shard_map/ppermute | solution.py:49
  82.2 3.9 %collective-permute-start.18 = (bf16[2048,256]{1,0:T(8,128)(2,1)S(1)}, bf16[2048,256]{1,0:T(8,128)(2,1)S(1)}, u32[]{:S(2)}, u32[]{:S(2)}) collective-permute-start(bf16[2048,256]{1,0:T(8,128)(2,1)S(1)} %pack.1.mine), channel_id=1, source_target_pairs={{0,1},{1,0},{2,3},{3,2},{4,5},{5,4},{6,7},{7,6},{8,9},{9,8},{10,11... | collective-permute-start | bytes 3145736 | tf_op jit(solution)/shard_map/ppermute | solution.py:49
  86.0 1.3 collective-permute-start.20
  87.3 3.0 %collective-permute-start.17 = (bf16[528,768]{1,0:T(8,128)(2,1)S(1)}, bf16[528,768]{1,0:T(8,128)(2,1)S(1)}, u32[]{:S(2)}, u32[]{:S(2)}) collective-permute-start(bf16[528,768]{1,0:T(8,128)(2,1)S(1)} %copy-done.10), channel_id=1, source_target_pairs={{0,1},{1,0},{2,3},{3,2},{4,5},{5,4},{6,7},{7,6},{8,9},{9,8},{10,11... | collective-permute-start | bytes 2433032 | tf_op jit(solution)/shard_map/ppermute | solution.py:49
  91.0 2.7 %collective-permute-start.24 = (bf16[256,1024]{1,0:T(8,128)(2,1)S(1)}, bf16[256,1024]{1,0:T(8,128)(2,1)S(1)}, u32[]{:S(2)}, u32[]{:S(2)}) collective-permute-start(bf16[256,1024]{1,0:T(8,128)(2,1)S(1)} %pad_maximum_fusion.10), channel_id=1, source_target_pairs={{0,6},{1,7},{2,0},{3,1},{4,2},{5,3},{6,4},{7,5},{8,14},{9,15},{10,... | collective-permute-start | bytes 1572872 | tf_op jit(solution)/shard_map/ppermute | solution.py:49
  94.0 1.7 collective-permute-start.22
  95.8 9.9 %decode_parts.1 = f32[8,32,384]{2,1,0:T(8,128)S(1)} custom-call(s32[8]{0:T(128)S(1)} %copy-done.7, s32[8]{0:T(128)S(1)} %copy-done.8, bf16[256,256]{1,0:T(8,128)(2,1)S(1)} %bitcast.73, bf16[128,4,16,256]{3,2,1,0:T(8,128)(2,1)} %keys.1, bf16[128,4,16,256]{3,2,1,0:T(8,128)(2,1)} %values.1, f32[8,1024]{1,0:T(8,128)S(1)} %reshape.39.ok_ref, ...), custom_call_target="tpu_custom_call" | custom-call | flops 536870912 | bytes 10485760 | tf_op jit(solution)/shard_map/decode_parts/pallas_call | solution.py:513
  105.7 1.2 collective-permute-start.19
  107.0 11.2 %attend_own.1 = (f32[4,512,256]{2,1,0:T(8,128)S(1)}, f32[4,512,128]{2,1,0:T(8,128)S(1)}) custom-call(s32[8]{0:T(128)S(1)} %copy-done.7, s32[8]{0:T(128)S(1)} %copy-done.8, bf16[544,384]{1,0:T(8,128)(2,1)S(1)} %get-tuple-element.75.a.q0.refs_0_, bf16[544,384]{1,0:T(8,128)(2,1)S(1)} %collective-permute-done.12.b.q1.refs_0_, ...), custom_call_target="tpu_custom_call" | custom-call | flops 2147483648 | bytes 4194304 | tf_op jit(solution)/shard_map/attend_own/pallas_call | solution.py:351
  118.2 1.8 collective-permute-start.21
  120.5 1.6 collective-permute-start.25
  122.0 1.1 collective-permute-start.26
  123.2 9.8 %attend_cross.2 = bf16[3,512,128]{2,1,0:T(8,128)(2,1)S(1)} custom-call(s32[8]{0:T(128)S(1)} %copy-done.7, s32[8]{0:T(128)S(1)} %copy-done.8, bf16[544,384]{1,0:T(8,128)(2,1)S(1)} %collective-permute-done.12.b.q1.refs_0_, bf16[544,384]{1,0:T(8,128)(2,1)S(1)} %collective-permute-done.14.c.q2.refs_1_, ...), custom_call_target="tpu_custom_call" | custom-call | flops 2147483648 | bytes 4194304 | tf_op jit(solution)/shard_map/attend_cross/pallas_call | solution.py:412
  133.1 1.8 collective-permute-start.36
  135.5 0.9 collective-permute-start.31
  136.5 3.0 %collective-permute-start.28 = (bf16[512,128]{1,0:T(8,128)(2,1)S(1)}, bf16[512,128]{1,0:T(8,128)(2,1)S(1)}, u32[]{:S(2)}, u32[]{:S(2)}) collective-permute-start(bf16[512,128]{1,0:T(8,128)(2,1)S(1)} %get-tuple-element.136), channel_id=1, source_target_pairs={{0,48},{1,49},{2,50},{3,51},{4,52},{5,53},{6,54},{7,55},{8,56},{9,... | collective-permute-start | bytes 393224 | tf_op jit(solution)/shard_map/ppermute | solution.py:49
  140.2 4.3 %attend_cross.3 = bf16[1,512,128]{2,1,0:T(8,128)(2,1)S(1)} custom-call(s32[8]{0:T(128)S(1)} %copy-done.7, s32[8]{0:T(128)S(1)} %copy-done.8, bf16[544,384]{1,0:T(8,128)(2,1)S(1)} %get-tuple-element.75.a.q0.refs_0_, bf16[2048,256]{1,0:T(8,128)(2,1)S(1)} %collective-permute-done.20.refs_3_.refs_1_, ...), custom_call_target="tpu_custom_call" | custom-call | flops 2147483648 | bytes 4194304 | tf_op jit(solution)/shard_map/attend_cross/pallas_call | solution.py:412
  145.1 0.7 collective-permute-done.29.c
  145.8 3.4 %collective-permute-done.30.d = bf16[512,128]{1,0:T(8,128)(2,1)S(1)} collective-permute-done((bf16[512,128]{1,0:T(8,128)(2,1)S(1)}, bf16[512,128]{1,0:T(8,128)(2,1)S(1)}, u32[]{:S(2)}, u32[]{:S(2)}) %collective-permute-start.30) | collective-permute-done | bytes 131104 | tf_op jit(solution)/shard_map/ppermute | solution.py:49
  150.4 1.5 collective-permute-start.33
  151.9 1.3 collective-permute-start.35
  153.2 4.0 %collective-permute-done.36.refs_6_.refs_5_.refs_4_ = bf16[1024,512]{1,0:T(8,128)(2,1)S(1)} collective-permute-done((bf16[1024,512]{1,0:T(8,128)(2,1)S(1)}, bf16[1024,512]{1,0:T(8,128)(2,1)S(1)}, u32[]{:S(2)}, u32[]{:S(2)}) %collective-permute-start.36) | collective-permute-done | bytes 1048608 | tf_op jit(solution)/shard_map/ppermute | solution.py:49
  157.2 3.3 %collective-permute-start.37 = (bf16[1024,512]{1,0:T(8,128)(2,1)S(1)}, bf16[1024,512]{1,0:T(8,128)(2,1)S(1)}, u32[]{:S(2)}, u32[]{:S(2)}) collective-permute-start(bf16[1024,512]{1,0:T(8,128)(2,1)S(1)} %collective-permute-done.36.refs_6_.refs_5_.refs_4_), channel_id=1, source_target_pairs={{0,1},{1,0},{2,3},{3,2},{4,5},{5,4},{6,7},{7,6},{8,9},{9,8},{10,11... | collective-permute-start | bytes 3145736 | tf_op jit(solution)/shard_map/ppermute | solution.py:49
  160.5 8.3 %collective-permute-done.34.refs_3_ = bf16[528,512]{1,0:T(8,128)(2,1)S(1)} collective-permute-done((bf16[528,512]{1,0:T(8,128)(2,1)S(1)}, bf16[528,512]{1,0:T(8,128)(2,1)S(1)}, u32[]{:S(2)}, u32[]{:S(2)}) %collective-permute-start.34) | collective-permute-done | bytes 540704 | tf_op jit(solution)/shard_map/ppermute | solution.py:49
  168.9 2.6 %collective-permute-start.39 = (bf16[544,512]{1,0:T(8,128)(2,1)S(1)}, bf16[544,512]{1,0:T(8,128)(2,1)S(1)}, u32[]{:S(2)}, u32[]{:S(2)}) collective-permute-start(bf16[544,512]{1,0:T(8,128)(2,1)S(1)} %pad_maximum_fusion.2), channel_id=1, source_target_pairs={{0,6},{1,7},{2,0},{3,1},{4,2},{5,3},{6,4},{7,5},{8,14},{9,15},{10,... | collective-permute-start | bytes 1671176 | tf_op jit(solution)/shard_map/ppermute | solution.py:49
  171.7 1.2 collective-permute-start.40
  172.9 1.8 out_project.3
  174.8 9.0 %collective-permute-done.40.refs_2_ = bf16[512,512]{1,0:T(8,128)(2,1)S(1)} collective-permute-done((bf16[512,512]{1,0:T(8,128)(2,1)S(1)}, bf16[512,512]{1,0:T(8,128)(2,1)S(1)}, u32[]{:S(2)}, u32[]{:S(2)}) %collective-permute-start.40) | collective-permute-done | bytes 524320 | tf_op jit(solution)/shard_map/ppermute | solution.py:49
  183.8 1.4 collective-permute-done.38.refs_0_
  185.3 1.1 collective-permute-start.42
  186.9 1.6 out_project.4
  188.4 4.4 %collective-permute-done.41.refs_0_ = bf16[256,512]{1,0:T(8,128)(2,1)S(1)} collective-permute-done((bf16[256,512]{1,0:T(8,128)(2,1)S(1)}, bf16[256,512]{1,0:T(8,128)(2,1)S(1)}, u32[]{:S(2)}, u32[]{:S(2)}) %collective-permute-start.41) | collective-permute-done | bytes 262176 | tf_op jit(solution)/shard_map/ppermute | solution.py:49
  192.8 1.0 out_project.5
  193.8 4.1 %collective-permute-start.43 = (f32[528,256]{1,0:T(8,128)S(1)}, f32[528,256]{1,0:T(8,128)S(1)}, u32[]{:S(2)}, u32[]{:S(2)}) collective-permute-start(f32[528,256]{1,0:T(8,128)S(1)} %get-tuple-element.117), channel_id=1, source_target_pairs={{0,1},{1,0},{2,3},{3,2},{4,5},{5,4},{6,7},{7,6},{8,9},{9,8},{10,11... | collective-permute-start | bytes 1622024 | tf_op jit(solution)/shard_map/ppermute | solution.py:49
  197.9 1.6 collective-permute-done.43
  199.8 1.0 copy.35
  (135 shorter events, 8.9 us)
Async XLA Ops:
  1.7 6.8 %copy-start = (bf16[4096,256]{1,0:T(8,128)(2,1)S(1)}, bf16[4096,256]{1,0:T(8,128)(2,1)}, u32[]{:S(2)}) copy-start(bf16[4096,256]{1,0:T(8,128)(2,1)} %refs_2_.1) | copy-start | bytes 6291460
  2.7 1.9 collective-permute-start
  4.7 17.6 %copy-start.11 = (bf16[528,512]{1,0:T(8,128)(2,1)}, bf16[528,512]{1,0:T(8,128)(2,1)S(1)}, u32[]{:S(2)}) copy-start(bf16[528,512]{1,0:T(8,128)(2,1)S(1)} %pad_maximum_fusion.3.refs_0_) | copy-start | bytes 1622020
  4.7 14.9 %collective-permute-start.1 = (bf16[528,512]{1,0:T(8,128)(2,1)S(1)}, bf16[528,512]{1,0:T(8,128)(2,1)S(1)}, u32[]{:S(2)}, u32[]{:S(2)}) collective-permute-start(bf16[528,512]{1,0:T(8,128)(2,1)S(1)} %pad_maximum_fusion.3.refs_0_), channel_id=1, source_target_pairs={{0,2},{1,3},{2,4},{3,5},{4,6},{5,7},{6,0},{7,1},{8,10},{9,11},{10,... | collective-permute-start | bytes 1622024 | tf_op jit(solution)/shard_map/ppermute | solution.py:49
  6.1 13.5 %collective-permute-start.2 = (bf16[528,512]{1,0:T(8,128)(2,1)S(1)}, bf16[528,512]{1,0:T(8,128)(2,1)S(1)}, u32[]{:S(2)}, u32[]{:S(2)}) collective-permute-start(bf16[528,512]{1,0:T(8,128)(2,1)S(1)} %pad_maximum_fusion.3.refs_0_), channel_id=1, source_target_pairs={{0,6},{1,7},{2,0},{3,1},{4,2},{5,3},{6,4},{7,5},{8,14},{9,15},{10,... | collective-permute-start | bytes 1622024 | tf_op jit(solution)/shard_map/ppermute | solution.py:49
  7.6 13.0 %collective-permute-start.3 = (bf16[528,512]{1,0:T(8,128)(2,1)S(1)}, bf16[528,512]{1,0:T(8,128)(2,1)S(1)}, u32[]{:S(2)}, u32[]{:S(2)}) collective-permute-start(bf16[528,512]{1,0:T(8,128)(2,1)S(1)} %pad_maximum_fusion.3.refs_0_), channel_id=1, source_target_pairs={{0,8},{1,9},{2,10},{3,11},{4,12},{5,13},{6,14},{7,15},{8,0},{9,1},... | collective-permute-start | bytes 1622024 | tf_op jit(solution)/shard_map/ppermute | solution.py:49
  8.5 18.0 %collective-permute-start.4 = (bf16[4096,256]{1,0:T(8,128)(2,1)S(1)}, bf16[4096,256]{1,0:T(8,128)(2,1)S(1)}, u32[]{:S(2)}, u32[]{:S(2)}) collective-permute-start(bf16[4096,256]{1,0:T(8,128)(2,1)S(1)} %copy-done), channel_id=1, source_target_pairs={{0,1},{1,0},{2,3},{3,2},{4,5},{5,4},{6,7},{7,6},{8,9},{9,8},{10,11... | collective-permute-start | bytes 6291464 | tf_op jit(solution)/shard_map/ppermute | solution.py:49
  9.6 19.8 %collective-permute-start.5 = (bf16[4096,256]{1,0:T(8,128)(2,1)}, bf16[4096,256]{1,0:T(8,128)(2,1)}, u32[]{:S(2)}, u32[]{:S(2)}) collective-permute-start(bf16[4096,256]{1,0:T(8,128)(2,1)} %refs_3_.3), channel_id=1, source_target_pairs={{0,1},{1,0},{2,3},{3,2},{4,5},{5,4},{6,7},{7,6},{8,9},{9,8},{10,11... | collective-permute-start | bytes 6291464 | tf_op jit(solution)/shard_map/ppermute | solution.py:49
  19.6 5.0 %copy-start.15 = (bf16[528,512]{1,0:T(8,128)(2,1)}, bf16[528,512]{1,0:T(8,128)(2,1)S(1)}, u32[]{:S(2)}) copy-start(bf16[528,512]{1,0:T(8,128)(2,1)S(1)} %collective-permute-done.1.refs_1_) | copy-start | bytes 1622020
  19.6 3.6 %copy-start.12 = (bf16[528,512]{1,0:T(8,128)(2,1)}, bf16[528,512]{1,0:T(8,128)(2,1)S(1)}, u32[]{:S(2)}) copy-start(bf16[528,512]{1,0:T(8,128)(2,1)S(1)} %collective-permute-done.2.refs_2_) | copy-start | bytes 1622020
  20.6 1.7 copy-start.14
  20.6 8.8 %collective-permute-start.6 = (bf16[4096,256]{1,0:T(8,128)(2,1)}, bf16[4096,256]{1,0:T(8,128)(2,1)}, u32[]{:S(2)}, u32[]{:S(2)}) collective-permute-start(bf16[4096,256]{1,0:T(8,128)(2,1)} %refs_4_.5), channel_id=1, source_target_pairs={{0,1},{1,0},{2,3},{3,2},{4,5},{5,4},{6,7},{7,6},{8,9},{9,8},{10,11... | collective-permute-start | bytes 6291464 | tf_op jit(solution)/shard_map/ppermute | solution.py:49
  23.2 16.9 %collective-permute-start.8 = (bf16[544,512]{1,0:T(8,128)(2,1)}, bf16[544,512]{1,0:T(8,128)(2,1)S(1)}, u32[]{:S(2)}, u32[]{:S(2)}) collective-permute-start(bf16[544,512]{1,0:T(8,128)(2,1)} %pad_maximum_fusion.1), channel_id=1, source_target_pairs={{0,6},{1,7},{2,0},{3,1},{4,2},{5,3},{6,4},{7,5},{8,14},{9,15},{10,... | collective-permute-start | bytes 1671176 | tf_op jit(solution)/shard_map/ppermute | solution.py:49
  24.6 1.0 slice-start
  25.5 14.6 %collective-permute-start.7 = (bf16[528,512]{1,0:T(8,128)(2,1)}, bf16[528,512]{1,0:T(8,128)(2,1)S(1)}, u32[]{:S(2)}, u32[]{:S(2)}) collective-permute-start(bf16[528,512]{1,0:T(8,128)(2,1)} %pad_maximum_fusion.4), channel_id=1, source_target_pairs={{0,2},{1,3},{2,4},{3,5},{4,6},{5,7},{6,0},{7,1},{8,10},{9,11},{10,... | collective-permute-start | bytes 1622024 | tf_op jit(solution)/shard_map/ppermute | solution.py:49
  26.4 1.3 copy-start.4
  27.8 12.3 %collective-permute-start.9 = (bf16[512,512]{1,0:T(8,128)(2,1)}, bf16[512,512]{1,0:T(8,128)(2,1)S(1)}, u32[]{:S(2)}, u32[]{:S(2)}) collective-permute-start(bf16[512,512]{1,0:T(8,128)(2,1)} %pad_maximum_fusion.6), channel_id=1, source_target_pairs={{0,8},{1,9},{2,10},{3,11},{4,12},{5,13},{6,14},{7,15},{8,0},{9,1},... | collective-permute-start | bytes 1572872 | tf_op jit(solution)/shard_map/ppermute | solution.py:49
  29.3 13.5 %copy-start.7 = (s32[8]{0:T(128)S(1)}, s32[8]{0:T(128)}, u32[]{:S(2)}) copy-start(s32[8]{0:T(128)} %stack.57.idx) | copy-start | bytes 100
  29.4 13.5 %copy-start.1 = (bf16[4096,256]{1,0:T(8,128)(2,1)S(1)}, bf16[4096,256]{1,0:T(8,128)(2,1)}, u32[]{:S(2)}) copy-start(bf16[4096,256]{1,0:T(8,128)(2,1)} %refs_2_.1) | copy-start | bytes 6291460
  29.4 13.5 %copy-start.2 = (bf16[4096,256]{1,0:T(8,128)(2,1)S(1)}, bf16[4096,256]{1,0:T(8,128)(2,1)}, u32[]{:S(2)}) copy-start(bf16[4096,256]{1,0:T(8,128)(2,1)} %refs_3_.3) | copy-start | bytes 6291460
  29.4 13.5 %copy-start.3 = (bf16[4096,256]{1,0:T(8,128)(2,1)S(1)}, bf16[4096,256]{1,0:T(8,128)(2,1)}, u32[]{:S(2)}) copy-start(bf16[4096,256]{1,0:T(8,128)(2,1)} %refs_4_.5) | copy-start | bytes 6291460
  40.1 12.1 %collective-permute-start.11 = (bf16[272,512]{1,0:T(8,128)(2,1)S(1)}, bf16[272,512]{1,0:T(8,128)(2,1)S(1)}, u32[]{:S(2)}, u32[]{:S(2)}) collective-permute-start(bf16[272,512]{1,0:T(8,128)(2,1)S(1)} %slice.136), channel_id=1, source_target_pairs={{0,6},{1,7},{2,0},{3,1},{4,2},{5,3},{6,4},{7,5},{8,14},{9,15},{10,... | collective-permute-start | bytes 835592 | tf_op jit(solution)/shard_map/ppermute | solution.py:49
  42.7 9.5 %collective-permute-start.10 = (bf16[256,512]{1,0:T(8,128)(2,1)S(1)}, bf16[256,512]{1,0:T(8,128)(2,1)S(1)}, u32[]{:S(2)}, u32[]{:S(2)}) collective-permute-start(bf16[256,512]{1,0:T(8,128)(2,1)S(1)} %slice.135), channel_id=1, source_target_pairs={{0,2},{1,3},{2,4},{3,5},{4,6},{5,7},{6,0},{7,1},{8,10},{9,11},{10,... | collective-permute-start | bytes 786440 | tf_op jit(solution)/shard_map/ppermute | solution.py:49
  42.9 1.6 copy-start.5
  44.5 20.4 %copy-start.16 = (s32[128,4]{0,1:T(4,128)S(1)}, s32[128,4]{0,1:T(4,128)}, u32[]{:S(2)}) copy-start(s32[128,4]{0,1:T(4,128)} %param.20) | copy-start | bytes 6148
  44.5 36.9 %copy-start.17 = (s32[128]{0:T(128)S(1)}, s32[128]{0:T(128)}, u32[]{:S(2)}) copy-start(s32[128]{0:T(128)} %param.21) | copy-start | bytes 1540
  52.2 1.9 copy-start.6
  58.9 0.9 copy-start.9
  59.8 11.3 %collective-permute-start.12 = (bf16[544,384]{1,0:T(8,128)(2,1)}, bf16[544,384]{1,0:T(8,128)(2,1)S(1)}, u32[]{:S(2)}, u32[]{:S(2)}) collective-permute-start(bf16[544,384]{1,0:T(8,128)(2,1)} %get-tuple-element.71), channel_id=1, source_target_pairs={{0,16},{1,17},{2,18},{3,19},{4,20},{5,21},{6,22},{7,23},{8,24},{9,... | collective-permute-start | bytes 1253384 | tf_op jit(solution)/shard_map/ppermute | solution.py:49
  61.4 9.7 %collective-permute-start.13 = (bf16[544,384]{1,0:T(8,128)(2,1)}, bf16[544,384]{1,0:T(8,128)(2,1)S(1)}, u32[]{:S(2)}, u32[]{:S(2)}) collective-permute-start(bf16[544,384]{1,0:T(8,128)(2,1)} %get-tuple-element.72), channel_id=1, source_target_pairs={{0,48},{1,49},{2,50},{3,51},{4,52},{5,53},{6,54},{7,55},{8,56},{9,... | collective-permute-start | bytes 1253384 | tf_op jit(solution)/shard_map/ppermute | solution.py:49
  63.6 17.4 %collective-permute-start.14 = (bf16[544,384]{1,0:T(8,128)(2,1)S(1)}, bf16[544,384]{1,0:T(8,128)(2,1)S(1)}, u32[]{:S(2)}, u32[]{:S(2)}) collective-permute-start(bf16[544,384]{1,0:T(8,128)(2,1)S(1)} %get-tuple-element.73), channel_id=1, source_target_pairs={{0,32},{1,33},{2,34},{3,35},{4,36},{5,37},{6,38},{7,39},{8,40},{9,... | collective-permute-start | bytes 1253384 | tf_op jit(solution)/shard_map/ppermute | solution.py:49
  81.0 6.3 %collective-permute-start.15 = (bf16[4,2,16,256]{3,2,1,0:T(8,128)(2,1)S(1)}, bf16[4,2,16,256]{3,2,1,0:T(8,128)(2,1)S(1)}, u32[]{:S(2)}, u32[]{:S(2)}) collective-permute-start(bf16[4,2,16,256]{3,2,1,0:T(8,128)(2,1)S(1)} %pad_maximum_fusion.17), channel_id=1, source_target_pairs={{0,64},{1,65},{2,66},{3,67},{4,68},{5,69},{6,70},{7,71},{8,72},{9,... | collective-permute-start | bytes 196616 | tf_op jit(solution)/shard_map/ppermute | solution.py:49
  82.1 5.3 %copy-start.10 = (bf16[528,768]{1,0:T(8,128)(2,1)S(1)}, bf16[528,768]{1,0:T(8,128)(2,1)}, u32[]{:S(2)}) copy-start(bf16[528,768]{1,0:T(8,128)(2,1)} %copy-done.9) | copy-start | bytes 2433028
  82.1 8.6 %copy-start.13 = (bf16[256,4096]{1,0:T(8,128)(2,1)S(1)}, bf16[256,4096]{1,0:T(8,128)(2,1)}, u32[]{:S(2)}) copy-start(bf16[256,4096]{1,0:T(8,128)(2,1)} %param.16) | copy-start | bytes 6291460
  82.2 23.6 %collective-permute-start.18 = (bf16[2048,256]{1,0:T(8,128)(2,1)S(1)}, bf16[2048,256]{1,0:T(8,128)(2,1)S(1)}, u32[]{:S(2)}, u32[]{:S(2)}) collective-permute-start(bf16[2048,256]{1,0:T(8,128)(2,1)S(1)} %pack.1.mine), channel_id=1, source_target_pairs={{0,1},{1,0},{2,3},{3,2},{4,5},{5,4},{6,7},{7,6},{8,9},{9,8},{10,11... | collective-permute-start | bytes 3145736 | tf_op jit(solution)/shard_map/ppermute | solution.py:49
  86.0 32.2 %collective-permute-start.20 = (bf16[2048,256]{1,0:T(8,128)(2,1)S(1)}, bf16[2048,256]{1,0:T(8,128)(2,1)S(1)}, u32[]{:S(2)}, u32[]{:S(2)}) collective-permute-start(bf16[2048,256]{1,0:T(8,128)(2,1)S(1)} %pack.1.mine), channel_id=1, source_target_pairs={{0,64},{1,65},{2,66},{3,67},{4,68},{5,69},{6,70},{7,71},{8,72},{9,... | collective-permute-start | bytes 3145736 | tf_op jit(solution)/shard_map/ppermute | solution.py:49
  87.3 6.7 %collective-permute-start.17 = (bf16[528,768]{1,0:T(8,128)(2,1)S(1)}, bf16[528,768]{1,0:T(8,128)(2,1)S(1)}, u32[]{:S(2)}, u32[]{:S(2)}) collective-permute-start(bf16[528,768]{1,0:T(8,128)(2,1)S(1)} %copy-done.10), channel_id=1, source_target_pairs={{0,1},{1,0},{2,3},{3,2},{4,5},{5,4},{6,7},{7,6},{8,9},{9,8},{10,11... | collective-permute-start | bytes 2433032 | tf_op jit(solution)/shard_map/ppermute | solution.py:49
  90.4 3.5 %collective-permute-start.16 = (bf16[8,16,256]{2,1,0:T(8,128)(2,1)S(1)}, bf16[8,16,256]{2,1,0:T(8,128)(2,1)S(1)}, u32[]{:S(2)}, u32[]{:S(2)}) collective-permute-start(bf16[8,16,256]{2,1,0:T(8,128)(2,1)S(1)} %slice_bitcast_fusion.4), channel_id=1, source_target_pairs={{0,1},{1,0},{2,3},{3,2},{4,5},{5,4},{6,7},{7,6},{8,9},{9,8},{10,11... | collective-permute-start | bytes 196616 | tf_op jit(solution)/shard_map/ppermute | solution.py:49
  91.0 29.1 %collective-permute-start.24 = (bf16[256,1024]{1,0:T(8,128)(2,1)S(1)}, bf16[256,1024]{1,0:T(8,128)(2,1)S(1)}, u32[]{:S(2)}, u32[]{:S(2)}) collective-permute-start(bf16[256,1024]{1,0:T(8,128)(2,1)S(1)} %pad_maximum_fusion.10), channel_id=1, source_target_pairs={{0,6},{1,7},{2,0},{3,1},{4,2},{5,3},{6,4},{7,5},{8,14},{9,15},{10,... | collective-permute-start | bytes 1572872 | tf_op jit(solution)/shard_map/ppermute | solution.py:49
  93.7 2.0 %copy-start.8 = (s32[8]{0:T(128)S(1)}, s32[8]{0:T(128)}, u32[]{:S(2)}) copy-start(s32[8]{0:T(128)} %lens.7) | copy-start | bytes 100
  93.9 26.3 %collective-permute-start.23 = (bf16[256,1024]{1,0:T(8,128)(2,1)S(1)}, bf16[256,1024]{1,0:T(8,128)(2,1)S(1)}, u32[]{:S(2)}, u32[]{:S(2)}) collective-permute-start(bf16[256,1024]{1,0:T(8,128)(2,1)S(1)} %pad_maximum_fusion.9), channel_id=1, source_target_pairs={{0,4},{1,5},{2,6},{3,7},{4,0},{5,1},{6,2},{7,3},{8,12},{9,13},{10,... | collective-permute-start | bytes 1572872 | tf_op jit(solution)/shard_map/ppermute | solution.py:49
  94.0 26.2 %collective-permute-start.22 = (bf16[256,1024]{1,0:T(8,128)(2,1)S(1)}, bf16[256,1024]{1,0:T(8,128)(2,1)S(1)}, u32[]{:S(2)}, u32[]{:S(2)}) collective-permute-start(bf16[256,1024]{1,0:T(8,128)(2,1)S(1)} %pad_maximum_fusion.8), channel_id=1, source_target_pairs={{0,2},{1,3},{2,4},{3,5},{4,6},{5,7},{6,0},{7,1},{8,10},{9,11},{10,... | collective-permute-start | bytes 1572872 | tf_op jit(solution)/shard_map/ppermute | solution.py:49
  105.7 12.5 %collective-permute-start.19 = (f32[4,32,384]{2,1,0:T(8,128)S(1)}, f32[4,32,384]{2,1,0:T(8,128)S(1)}, u32[]{:S(2)}, u32[]{:S(2)}) collective-permute-start(f32[4,32,384]{2,1,0:T(8,128)S(1)} %slice.174), channel_id=1, source_target_pairs={{0,64},{1,65},{2,66},{3,67},{4,68},{5,69},{6,70},{7,71},{8,72},{9,... | collective-permute-start | bytes 589832 | tf_op jit(solution)/shard_map/ppermute | solution.py:49
  118.2 4.9 %collective-permute-start.21 = (bf16[2048,256]{1,0:T(8,128)(2,1)S(1)}, bf16[2048,256]{1,0:T(8,128)(2,1)S(1)}, u32[]{:S(2)}, u32[]{:S(2)}) collective-permute-start(bf16[2048,256]{1,0:T(8,128)(2,1)S(1)} %collective-permute-done.20.refs_3_.refs_1_), channel_id=1, source_target_pairs={{0,1},{1,0},{2,3},{3,2},{4,5},{5,4},{6,7},{7,6},{8,9},{9,8},{10,11... | collective-permute-start | bytes 3145736 | tf_op jit(solution)/shard_map/ppermute | solution.py:49
  120.5 12.6 %collective-permute-start.25 = (f32[2,32,384]{2,1,0:T(8,128)S(1)}, f32[2,32,384]{2,1,0:T(8,128)S(1)}, u32[]{:S(2)}, u32[]{:S(2)}) collective-permute-start(f32[2,32,384]{2,1,0:T(8,128)S(1)} %get-tuple-element.138), channel_id=1, source_target_pairs={{0,48},{1,49},{2,50},{3,51},{4,52},{5,53},{6,54},{7,55},{8,56},{9,... | collective-permute-start | bytes 294920 | tf_op jit(solution)/shard_map/ppermute | solution.py:49
  122.0 11.0 %collective-permute-start.26 = (f32[2,32,384]{2,1,0:T(8,128)S(1)}, f32[2,32,384]{2,1,0:T(8,128)S(1)}, u32[]{:S(2)}, u32[]{:S(2)}) collective-permute-start(f32[2,32,384]{2,1,0:T(8,128)S(1)} %get-tuple-element.140), channel_id=1, source_target_pairs={{0,32},{1,33},{2,34},{3,35},{4,36},{5,37},{6,38},{7,39},{8,40},{9,... | collective-permute-start | bytes 294920 | tf_op jit(solution)/shard_map/ppermute | solution.py:49
  123.2 9.9 %collective-permute-start.27 = (f32[2,32,384]{2,1,0:T(8,128)S(1)}, f32[2,32,384]{2,1,0:T(8,128)S(1)}, u32[]{:S(2)}, u32[]{:S(2)}) collective-permute-start(f32[2,32,384]{2,1,0:T(8,128)S(1)} %get-tuple-element.139), channel_id=1, source_target_pairs={{0,16},{1,17},{2,18},{3,19},{4,20},{5,21},{6,22},{7,23},{8,24},{9,... | collective-permute-start | bytes 294920 | tf_op jit(solution)/shard_map/ppermute | solution.py:49
  133.1 24.1 %collective-permute-start.36 = (bf16[1024,512]{1,0:T(8,128)(2,1)S(1)}, bf16[1024,512]{1,0:T(8,128)(2,1)S(1)}, u32[]{:S(2)}, u32[]{:S(2)}) collective-permute-start(bf16[1024,512]{1,0:T(8,128)(2,1)S(1)} %get-tuple-element.106), channel_id=1, source_target_pairs={{0,8},{1,9},{2,10},{3,11},{4,12},{5,13},{6,14},{7,15},{8,0},{9,1},... | collective-permute-start | bytes 3145736 | tf_op jit(solution)/shard_map/ppermute | solution.py:49
  135.5 9.0 %collective-permute-start.31 = (bf16[16,256]{1,0:T(8,128)(2,1)S(1)}, bf16[16,256]{1,0:T(8,128)(2,1)S(1)}, u32[]{:S(2)}, u32[]{:S(2)}) collective-permute-start(bf16[16,256]{1,0:T(8,128)(2,1)S(1)} %slice_select_fusion), channel_id=1, source_target_pairs={{0,1},{1,0},{2,3},{3,2},{4,5},{5,4},{6,7},{7,6},{8,9},{9,8},{10,11... | collective-permute-start | bytes 24584 | tf_op jit(solution)/shard_map/ppermute | solution.py:49
  136.5 8.6 %collective-permute-start.28 = (bf16[512,128]{1,0:T(8,128)(2,1)S(1)}, bf16[512,128]{1,0:T(8,128)(2,1)S(1)}, u32[]{:S(2)}, u32[]{:S(2)}) collective-permute-start(bf16[512,128]{1,0:T(8,128)(2,1)S(1)} %get-tuple-element.136), channel_id=1, source_target_pairs={{0,48},{1,49},{2,50},{3,51},{4,52},{5,53},{6,54},{7,55},{8,56},{9,... | collective-permute-start | bytes 393224 | tf_op jit(solution)/shard_map/ppermute | solution.py:49
  139.5 6.3 %collective-permute-start.29 = (bf16[512,128]{1,0:T(8,128)(2,1)S(1)}, bf16[512,128]{1,0:T(8,128)(2,1)S(1)}, u32[]{:S(2)}, u32[]{:S(2)}) collective-permute-start(bf16[512,128]{1,0:T(8,128)(2,1)S(1)} %get-tuple-element.135), channel_id=1, source_target_pairs={{0,32},{1,33},{2,34},{3,35},{4,36},{5,37},{6,38},{7,39},{8,40},{9,... | collective-permute-start | bytes 393224 | tf_op jit(solution)/shard_map/ppermute | solution.py:49
  140.1 9.1 %collective-permute-start.30 = (bf16[512,128]{1,0:T(8,128)(2,1)S(1)}, bf16[512,128]{1,0:T(8,128)(2,1)S(1)}, u32[]{:S(2)}, u32[]{:S(2)}) collective-permute-start(bf16[512,128]{1,0:T(8,128)(2,1)S(1)} %get-tuple-element.134), channel_id=1, source_target_pairs={{0,16},{1,17},{2,18},{3,19},{4,20},{5,21},{6,22},{7,23},{8,24},{9,... | collective-permute-start | bytes 393224 | tf_op jit(solution)/shard_map/ppermute | solution.py:49
  149.9 18.8 %collective-permute-start.34 = (bf16[528,512]{1,0:T(8,128)(2,1)S(1)}, bf16[528,512]{1,0:T(8,128)(2,1)S(1)}, u32[]{:S(2)}, u32[]{:S(2)}) collective-permute-start(bf16[528,512]{1,0:T(8,128)(2,1)S(1)} %head_order.1.refs_0_), channel_id=1, source_target_pairs={{0,8},{1,9},{2,10},{3,11},{4,12},{5,13},{6,14},{7,15},{8,0},{9,1},... | collective-permute-start | bytes 1622024 | tf_op jit(solution)/shard_map/ppermute | solution.py:49
  150.4 18.4 %collective-permute-start.33 = (bf16[528,512]{1,0:T(8,128)(2,1)S(1)}, bf16[528,512]{1,0:T(8,128)(2,1)S(1)}, u32[]{:S(2)}, u32[]{:S(2)}) collective-permute-start(bf16[528,512]{1,0:T(8,128)(2,1)S(1)} %head_order.1.refs_0_), channel_id=1, source_target_pairs={{0,6},{1,7},{2,0},{3,1},{4,2},{5,3},{6,4},{7,5},{8,14},{9,15},{10,... | collective-permute-start | bytes 1622024 | tf_op jit(solution)/shard_map/ppermute | solution.py:49
  151.9 19.6 %collective-permute-start.32 = (bf16[528,512]{1,0:T(8,128)(2,1)S(1)}, bf16[528,512]{1,0:T(8,128)(2,1)S(1)}, u32[]{:S(2)}, u32[]{:S(2)}) collective-permute-start(bf16[528,512]{1,0:T(8,128)(2,1)S(1)} %head_order.1.refs_0_), channel_id=1, source_target_pairs={{0,2},{1,3},{2,4},{3,5},{4,6},{5,7},{6,0},{7,1},{8,10},{9,11},{10,... | collective-permute-start | bytes 1622024 | tf_op jit(solution)/shard_map/ppermute | solution.py:49
  151.9 21.1 %collective-permute-start.35 = (bf16[1024,512]{1,0:T(8,128)(2,1)S(1)}, bf16[1024,512]{1,0:T(8,128)(2,1)S(1)}, u32[]{:S(2)}, u32[]{:S(2)}) collective-permute-start(bf16[1024,512]{1,0:T(8,128)(2,1)S(1)} %get-tuple-element.105.refs_4_.refs_3_.refs_2_), channel_id=1, source_target_pairs={{0,1},{1,0},{2,3},{3,2},{4,5},{5,4},{6,7},{7,6},{8,9},{9,8},{10,11... | collective-permute-start | bytes 3145736 | tf_op jit(solution)/shard_map/ppermute | solution.py:49
  157.2 15.8 %collective-permute-start.37 = (bf16[1024,512]{1,0:T(8,128)(2,1)S(1)}, bf16[1024,512]{1,0:T(8,128)(2,1)S(1)}, u32[]{:S(2)}, u32[]{:S(2)}) collective-permute-start(bf16[1024,512]{1,0:T(8,128)(2,1)S(1)} %collective-permute-done.36.refs_6_.refs_5_.refs_4_), channel_id=1, source_target_pairs={{0,1},{1,0},{2,3},{3,2},{4,5},{5,4},{6,7},{7,6},{8,9},{9,8},{10,11... | collective-permute-start | bytes 3145736 | tf_op jit(solution)/shard_map/ppermute | solution.py:49
  168.9 16.4 %collective-permute-start.39 = (bf16[544,512]{1,0:T(8,128)(2,1)S(1)}, bf16[544,512]{1,0:T(8,128)(2,1)S(1)}, u32[]{:S(2)}, u32[]{:S(2)}) collective-permute-start(bf16[544,512]{1,0:T(8,128)(2,1)S(1)} %pad_maximum_fusion.2), channel_id=1, source_target_pairs={{0,6},{1,7},{2,0},{3,1},{4,2},{5,3},{6,4},{7,5},{8,14},{9,15},{10,... | collective-permute-start | bytes 1671176 | tf_op jit(solution)/shard_map/ppermute | solution.py:49
  171.6 13.7 %collective-permute-start.38 = (bf16[528,512]{1,0:T(8,128)(2,1)S(1)}, bf16[528,512]{1,0:T(8,128)(2,1)S(1)}, u32[]{:S(2)}, u32[]{:S(2)}) collective-permute-start(bf16[528,512]{1,0:T(8,128)(2,1)S(1)} %pad_maximum_fusion.5), channel_id=1, source_target_pairs={{0,2},{1,3},{2,4},{3,5},{4,6},{5,7},{6,0},{7,1},{8,10},{9,11},{10,... | collective-permute-start | bytes 1622024 | tf_op jit(solution)/shard_map/ppermute | solution.py:49
  171.7 12.1 %collective-permute-start.40 = (bf16[512,512]{1,0:T(8,128)(2,1)S(1)}, bf16[512,512]{1,0:T(8,128)(2,1)S(1)}, u32[]{:S(2)}, u32[]{:S(2)}) collective-permute-start(bf16[512,512]{1,0:T(8,128)(2,1)S(1)} %pad_maximum_fusion.11), channel_id=1, source_target_pairs={{0,8},{1,9},{2,10},{3,11},{4,12},{5,13},{6,14},{7,15},{8,0},{9,1},... | collective-permute-start | bytes 1572872 | tf_op jit(solution)/shard_map/ppermute | solution.py:49
  185.3 7.6 %collective-permute-start.42 = (bf16[272,512]{1,0:T(8,128)(2,1)S(1)}, bf16[272,512]{1,0:T(8,128)(2,1)S(1)}, u32[]{:S(2)}, u32[]{:S(2)}) collective-permute-start(bf16[272,512]{1,0:T(8,128)(2,1)S(1)} %slice.163), channel_id=1, source_target_pairs={{0,6},{1,7},{2,0},{3,1},{4,2},{5,3},{6,4},{7,5},{8,14},{9,15},{10,... | collective-permute-start | bytes 835592 | tf_op jit(solution)/shard_map/ppermute | solution.py:49
  186.3 6.5 %collective-permute-start.41 = (bf16[256,512]{1,0:T(8,128)(2,1)S(1)}, bf16[256,512]{1,0:T(8,128)(2,1)S(1)}, u32[]{:S(2)}, u32[]{:S(2)}) collective-permute-start(bf16[256,512]{1,0:T(8,128)(2,1)S(1)} %slice.162), channel_id=1, source_target_pairs={{0,2},{1,3},{2,4},{3,5},{4,6},{5,7},{6,0},{7,1},{8,10},{9,11},{10,... | collective-permute-start | bytes 786440 | tf_op jit(solution)/shard_map/ppermute | solution.py:49
  193.8 5.7 %collective-permute-start.43 = (f32[528,256]{1,0:T(8,128)S(1)}, f32[528,256]{1,0:T(8,128)S(1)}, u32[]{:S(2)}, u32[]{:S(2)}) collective-permute-start(f32[528,256]{1,0:T(8,128)S(1)} %get-tuple-element.117), channel_id=1, source_target_pairs={{0,1},{1,0},{2,3},{3,2},{4,5},{5,4},{6,7},{7,6},{8,9},{9,8},{10,11... | collective-permute-start | bytes 1622024 | tf_op jit(solution)/shard_map/ppermute | solution.py:49
where the time goes:
time: 202 us; the launch traced here: 201 us
  Pallas kernels  63.7 us (32%)
  waiting for transfers between devices  62.3 us (31%)
  starting transfers between devices  59.1 us (29%)
  local copies, waits for them, and re-layouts  10.4 us (5%)
  other arithmetic  4.32 us (2%)
    ppermute x44, waiting for transfers between devices, move(): return lax.ppermute(x, AX, perm(**steps))  62.3 us
    ppermute x44, starting transfers between devices, move(): return lax.ppermute(x, AX, perm(**steps))  59.1 us
    pallas_call x3, Pallas kernels, qkv(): pl.pallas_call(functools.partial(qkv_kernel, step), out_shape=shape, in_s...  22.6 us
    pallas_call x2, Pallas kernels, attend_cross(): pl.pallas_call(functools.partial(attend_cross_kernel, which), out_shape=j...  14.1 us
    pallas_call x1, Pallas kernels, attend_own(): pl.pallas_call(attend_own_kernel, out_shape=(jax.ShapeDtypeStruct((4, HAL...  11.2 us
    pallas_call x1, Pallas kernels, decode_parts(): pl.pallas_call(decode_kernel, out_shape=jax.ShapeDtypeStruct((8, 32, 384)...  9.95 us
    unnamed x37, local copies, waits for them, and re-layouts  5.77 us
    pallas_call x3, Pallas kernels, out_project(): pl.pallas_call(functools.partial(out_kernel, step), out_shape=(jax.ShapeD...  4.38 us
  transfers between devices with their start and end apart: 44, of which 16 were waited for; matrix products, arithmetic and copies ran while one was open for 2% of the time, Pallas kernels for 29%

commit v1 on v0

--- a/solution.py
+++ b/solution.py
@@ -730,12 +730,14 @@
     moved = move(parts[4:], dxh=1)
     parts, mine = lax.optimization_barrier((parts, mine))
     state = attend_own(idx, stretch_lengths, blocks, mine, sib)
-    *state, moved, cross = lax.optimization_barrier((*state, moved, cross))
+    acc, top, *spread = lax.optimization_barrier((*state, *spread))
+    acc, top, moved, cross, near, far = lax.optimization_barrier(
+        (acc, top, moved, cross, *pack_weight(spread))
+    )
+    state = (acc, top)
     cross_sib = move(cross, dc=1)
     parts = jnp.stack([parts[:4], moved])
     moved = [move(parts[:, k], dz=4 - k) for k in (1, 2, 3)]
-    near, far = pack_weight(spread)
-    cross_sib, near, far = lax.optimization_barrier((cross_sib, near, far))
     far = move(far, dxl=1)
     first_heads = attend_cross(
         (1, 2, 3), idx, stretch_lengths, blocks[1:], cross, cross_sib, state

time: 202 us -> 200 us (0.990)
  starting transfers between devices: 59.1 us -> 52.5 us
  Pallas kernels: 63.7 us -> 65.9 us
    ppermute x44, starting transfers between devices: 59.1 us -> 52.5 us  [move(): return lax.ppermute(x, AX, perm(**steps))]
    pallas_call x2, Pallas kernels: 14.1 us -> 17.7 us  [attend_cross(): pl.pallas_call(functools.partial(attend_cross_kernel, which), out_shape=j...]
    unnamed x37 -> x35, local copies, waits for them, and re-layouts: 5.77 us -> 5.75 us
  transfers between devices with their start and end apart: 44 -> 44, of which waited for: 16 -> 15; matrix products, arithmetic and copies ran while one was open for 2% -> 4% of each run, Pallas kernels for 29% -> 30%
where the time goes in v1:
time: 200 us; the launch traced here: 201 us
  Pallas kernels  65.9 us (33%)
  waiting for transfers between devices  63.6 us (32%)
  starting transfers between devices  52.5 us (26%)
  local copies, waits for them, and re-layouts  11.8 us (6%)
  other arithmetic  5.93 us (3%)
    ppermute x44, waiting for transfers between devices, move(): return lax.ppermute(x, AX, perm(**steps))  63.6 us
    ppermute x44, starting transfers between devices, move(): return lax.ppermute(x, AX, perm(**steps))  52.5 us
    pallas_call x3, Pallas kernels, qkv(): pl.pallas_call(functools.partial(qkv_kernel, step), out_shape=shape, in_s...  22.6 us
    pallas_call x2, Pallas kernels, attend_cross(): pl.pallas_call(functools.partial(attend_cross_kernel, which), out_shape=j...  17.7 us
    pallas_call x1, Pallas kernels, decode_parts(): pl.pallas_call(decode_kernel, out_shape=jax.ShapeDtypeStruct((8, 32, 384)...  9.95 us
    pallas_call x1, Pallas kernels, attend_own(): pl.pallas_call(attend_own_kernel, out_shape=(jax.ShapeDtypeStruct((4, HAL...  9.82 us
    unnamed x35, local copies, waits for them, and re-layouts  5.75 us
    pallas_call x3, Pallas kernels, out_project(): pl.pallas_call(functools.partial(out_kernel, step), out_shape=(jax.ShapeD...  4.39 us
  transfers between devices with their start and end apart: 44, of which 15 were waited for; matrix products, arithmetic and copies ran while one was open for 4% of the time, Pallas kernels for 30%

profile of v1, /device:TPU:5, one launch (start us, length us, event | category | flops | bytes accessed | tf_op | source)
XLA Modules:
  0.0 201.3 jit_solution(17312299104689534969)
XLA Ops:
  0.6 1.1 fusion.8
  1.7 0.9 slice_bitcast_fusion.9
  2.7 0.8 collective-permute-start
  3.5 1.2 collective-permute-done
  4.7 1.4 collective-permute-start.1
  6.1 1.5 collective-permute-start.2
  7.6 0.9 collective-permute-start.3
  8.5 1.1 collective-permute-start.4
  9.6 10.0 %collective-permute-done.1.refs_1_ = bf16[528,512]{1,0:T(8,128)(2,1)S(1)} collective-permute-done((bf16[528,512]{1,0:T(8,128)(2,1)S(1)}, bf16[528,512]{1,0:T(8,128)(2,1)S(1)}, u32[]{:S(2)}, u32[]{:S(2)}) %collective-permute-start.1) | collective-permute-done | bytes 540704 | tf_op jit(solution)/shard_map/ppermute | solution.py:49
  19.6 1.0 collective-permute-done.3.refs_3_
  20.6 1.7 collective-permute-start.6
  22.3 0.8 pad_maximum_fusion.1
  23.2 1.4 collective-permute-start.8
  24.6 0.9 pad_maximum_fusion.4
  25.6 0.9 pad_maximum_fusion.6
  26.4 1.3 copy-done.4
  27.7 0.9 collective-permute-start.9
  29.4 10.1 %qkv.3.refs_9_ = f32[6,528,256]{2,1,0:T(8,128)} custom-call(s32[8]{0:T(128)} %stack.57.idx, bf16[528,512]{1,0:T(8,128)(2,1)} %copy-done.11, bf16[528,512]{1,0:T(8,128)(2,1)} %copy-done.14, bf16[528,512]{1,0:T(8,128)(2,1)} %copy-done.12, bf16[528,512]{1,0:T(8,128)(2,1)} %copy-done.13, bf16[4096,256]{1,0:T(8,128)(2,1)} %refs_2_.1, bf16[4096,256]{1,0:T(8,128)(2,1)} %refs_3_.3, ...), custom_call_target="tpu_custom_call" | custom-call | flops 3321888768 | bytes 8388608 | tf_op jit(solution)/shard_map/qkv/pallas_call | solution.py:187
  40.1 2.6 %collective-permute-start.11 = (bf16[272,512]{1,0:T(8,128)(2,1)S(1)}, bf16[272,512]{1,0:T(8,128)(2,1)S(1)}, u32[]{:S(2)}, u32[]{:S(2)}) collective-permute-start(bf16[272,512]{1,0:T(8,128)(2,1)S(1)} %slice.136), channel_id=1, source_target_pairs={{0,6},{1,7},{2,0},{3,1},{4,2},{5,3},{6,4},{7,5},{8,14},{9,15},{10,... | collective-permute-start | bytes 835592 | tf_op jit(solution)/shard_map/ppermute | solution.py:49
  42.8 1.6 copy-done.5
  44.4 7.7 %qkv.4.refs_8_ = f32[6,528,256]{2,1,0:T(8,128)} custom-call(s32[8]{0:T(128)S(1)} %copy-done.7, bf16[528,512]{1,0:T(8,128)(2,1)S(1)} %collective-permute-done.7.refs_0_, bf16[544,512]{1,0:T(8,128)(2,1)S(1)} %collective-permute-done.8.refs_1_, bf16[512,512]{1,0:T(8,128)(2,1)S(1)} %collective-permute-done.9.refs_2_, bf16[4096,256]{1,0:T(8,128)(2,1)S(1)} %copy-done.1, ...), custom_call_target="tpu_custom_call" | custom-call | flops 2491416576 | bytes 8388608 | tf_op jit(solution)/shard_map/qkv/pallas_call | solution.py:187
  52.2 1.9 copy-done.6
  54.1 4.8 %qkv.5 = (bf16[528,768]{1,0:T(8,128)(2,1)S(1)}, bf16[544,384]{1,0:T(8,128)(2,1)S(1)}, bf16[544,384]{1,0:T(8,128)(2,1)}, bf16[544,384]{1,0:T(8,128)(2,1)S(1)}, bf...) custom-call(s32[8]{0:T(128)S(1)} %copy-done.7, bf16[256,512]{1,0:T(8,128)(2,1)S(1)} %collective-permute-done.10.refs_0_, ...), custom_call_target="tpu_custom_call" | custom-call | flops 830472192 | bytes 8388608 | tf_op jit(solution)/shard_map/qkv/pallas_call | solution.py:187
  58.9 0.9 copy-done.9
  59.8 1.6 collective-permute-start.12
  61.4 2.1 %collective-permute-start.13 = (bf16[544,384]{1,0:T(8,128)(2,1)}, bf16[544,384]{1,0:T(8,128)(2,1)S(1)}, u32[]{:S(2)}, u32[]{:S(2)}) collective-permute-start(bf16[544,384]{1,0:T(8,128)(2,1)} %get-tuple-element.77), channel_id=1, source_target_pairs={{0,48},{1,49},{2,50},{3,51},{4,52},{5,53},{6,54},{7,55},{8,56},{9,... | collective-permute-start | bytes 1253384 | tf_op jit(solution)/shard_map/ppermute | solution.py:49
  63.5 1.3 collective-permute-start.14
  65.0 6.2 %collective-permute-done.12.b.q1.refs_0_ = bf16[544,384]{1,0:T(8,128)(2,1)S(1)} collective-permute-done((bf16[544,384]{1,0:T(8,128)(2,1)}, bf16[544,384]{1,0:T(8,128)(2,1)S(1)}, u32[]{:S(2)}, u32[]{:S(2)}) %collective-permute-start.12) | collective-permute-done | bytes 417824 | tf_op jit(solution)/shard_map/ppermute | solution.py:49
  71.1 9.8 %collective-permute-done.14.c.q2.refs_1_ = bf16[544,384]{1,0:T(8,128)(2,1)S(1)} collective-permute-done((bf16[544,384]{1,0:T(8,128)(2,1)S(1)}, bf16[544,384]{1,0:T(8,128)(2,1)S(1)}, u32[]{:S(2)}, u32[]{:S(2)}) %collective-permute-start.14) | collective-permute-done | bytes 417824 | tf_op jit(solution)/shard_map/ppermute | solution.py:49
  82.1 3.9 %collective-permute-start.18 = (bf16[2048,256]{1,0:T(8,128)(2,1)S(1)}, bf16[2048,256]{1,0:T(8,128)(2,1)S(1)}, u32[]{:S(2)}, u32[]{:S(2)}) collective-permute-start(bf16[2048,256]{1,0:T(8,128)(2,1)S(1)} %pack.1.mine), channel_id=1, source_target_pairs={{0,1},{1,0},{2,3},{3,2},{4,5},{5,4},{6,7},{7,6},{8,9},{9,8},{10,11... | collective-permute-start | bytes 3145736 | tf_op jit(solution)/shard_map/ppermute | solution.py:49
  86.0 1.3 collective-permute-start.23
  87.3 3.1 %collective-permute-start.17 = (bf16[528,768]{1,0:T(8,128)(2,1)S(1)}, bf16[528,768]{1,0:T(8,128)(2,1)S(1)}, u32[]{:S(2)}, u32[]{:S(2)}) collective-permute-start(bf16[528,768]{1,0:T(8,128)(2,1)S(1)} %copy-done.10), channel_id=1, source_target_pairs={{0,1},{1,0},{2,3},{3,2},{4,5},{5,4},{6,7},{7,6},{8,9},{9,8},{10,11... | collective-permute-start | bytes 2433032 | tf_op jit(solution)/shard_map/ppermute | solution.py:49
  90.4 1.7 constant_dynamic-slice_fusion.1
  92.1 2.7 %collective-permute-start.21 = (bf16[256,1024]{1,0:T(8,128)(2,1)S(1)}, bf16[256,1024]{1,0:T(8,128)(2,1)S(1)}, u32[]{:S(2)}, u32[]{:S(2)}) collective-permute-start(bf16[256,1024]{1,0:T(8,128)(2,1)S(1)} %pad_maximum_fusion.10), channel_id=1, source_target_pairs={{0,6},{1,7},{2,0},{3,1},{4,2},{5,3},{6,4},{7,5},{8,14},{9,15},{10,... | collective-permute-start | bytes 1572872 | tf_op jit(solution)/shard_map/ppermute | solution.py:49
  95.2 0.9 pad_maximum_fusion.9
  96.1 0.9 pad_maximum_fusion.8
  97.5 10.0 %decode_parts.1 = f32[8,32,384]{2,1,0:T(8,128)S(1)} custom-call(s32[8]{0:T(128)S(1)} %copy-done.7, s32[8]{0:T(128)S(1)} %copy-done.8, bf16[256,256]{1,0:T(8,128)(2,1)S(1)} %bitcast.73, bf16[128,4,16,256]{3,2,1,0:T(8,128)(2,1)} %keys.1, bf16[128,4,16,256]{3,2,1,0:T(8,128)(2,1)} %values.1, f32[8,1024]{1,0:T(8,128)S(1)} %reshape.39.ok_ref, ...), custom_call_target="tpu_custom_call" | custom-call | flops 536870912 | bytes 10485760 | tf_op jit(solution)/shard_map/decode_parts/pallas_call | solution.py:513
  107.5 1.4 collective-permute-start.22
  109.0 9.8 %attend_own.1 = (f32[4,512,256]{2,1,0:T(8,128)S(1)}, f32[4,512,128]{2,1,0:T(8,128)S(1)}) custom-call(s32[8]{0:T(128)S(1)} %copy-done.7, s32[8]{0:T(128)S(1)} %copy-done.8, bf16[544,384]{1,0:T(8,128)(2,1)S(1)} %get-tuple-element.80.a.q0.refs_0_, bf16[544,384]{1,0:T(8,128)(2,1)S(1)} %collective-permute-done.12.b.q1.refs_0_, ...), custom_call_target="tpu_custom_call" | custom-call | flops 2147483648 | bytes 4194304 | tf_op jit(solution)/shard_map/attend_own/pallas_call | solution.py:351
  118.8 4.7 %collective-permute-done.19.b = bf16[256,1024]{1,0:T(8,128)(2,1)S(1)} collective-permute-done((bf16[256,1024]{1,0:T(8,128)(2,1)}, bf16[256,1024]{1,0:T(8,128)(2,1)S(1)}, u32[]{:S(2)}, u32[]{:S(2)}) %collective-permute-start.19) | collective-permute-done | bytes 524320 | tf_op jit(solution)/shard_map/ppermute | solution.py:49
  123.7 0.8 collective-permute-start.24
  124.5 1.6 collective-permute-start.25
  126.1 1.1 collective-permute-start.26
  127.3 0.9 collective-permute-start.36
  128.2 12.5 %attend_cross.2 = bf16[3,512,128]{2,1,0:T(8,128)(2,1)S(1)} custom-call(s32[8]{0:T(128)S(1)} %copy-done.7, s32[8]{0:T(128)S(1)} %copy-done.8, bf16[544,384]{1,0:T(8,128)(2,1)S(1)} %collective-permute-done.12.b.q1.refs_0_, bf16[544,384]{1,0:T(8,128)(2,1)S(1)} %collective-permute-done.14.c.q2.refs_1_, ...), custom_call_target="tpu_custom_call" | custom-call | flops 2147483648 | bytes 4194304 | tf_op jit(solution)/shard_map/attend_cross/pallas_call | solution.py:412
  141.4 0.9 collective-permute-start.31
  142.4 3.0 %collective-permute-start.28 = (bf16[512,128]{1,0:T(8,128)(2,1)S(1)}, bf16[512,128]{1,0:T(8,128)(2,1)S(1)}, u32[]{:S(2)}, u32[]{:S(2)}) collective-permute-start(bf16[512,128]{1,0:T(8,128)(2,1)S(1)} %get-tuple-element.146), channel_id=1, source_target_pairs={{0,48},{1,49},{2,50},{3,51},{4,52},{5,53},{6,54},{7,55},{8,56},{9,... | collective-permute-start | bytes 393224 | tf_op jit(solution)/shard_map/ppermute | solution.py:49
  146.1 5.2 %attend_cross.3 = bf16[1,512,128]{2,1,0:T(8,128)(2,1)S(1)} custom-call(s32[8]{0:T(128)S(1)} %copy-done.7, s32[8]{0:T(128)S(1)} %copy-done.8, bf16[544,384]{1,0:T(8,128)(2,1)S(1)} %get-tuple-element.80.a.q0.refs_0_, bf16[2048,256]{1,0:T(8,128)(2,1)S(1)} %collective-permute-done.23.refs_3_.refs_1_, ...), custom_call_target="tpu_custom_call" | custom-call | flops 2147483648 | bytes 4194304 | tf_op jit(solution)/shard_map/attend_cross/pallas_call | solution.py:412
  151.7 3.4 %collective-permute-done.30.d = bf16[512,128]{1,0:T(8,128)(2,1)S(1)} collective-permute-done((bf16[512,128]{1,0:T(8,128)(2,1)S(1)}, bf16[512,128]{1,0:T(8,128)(2,1)S(1)}, u32[]{:S(2)}, u32[]{:S(2)}) %collective-permute-start.30) | collective-permute-done | bytes 131104 | tf_op jit(solution)/shard_map/ppermute | solution.py:49
  157.0 0.9 collective-permute-start.32
  157.9 1.3 collective-permute-start.37
  159.2 10.0 %collective-permute-done.34.refs_3_ = bf16[528,512]{1,0:T(8,128)(2,1)S(1)} collective-permute-done((bf16[528,512]{1,0:T(8,128)(2,1)S(1)}, bf16[528,512]{1,0:T(8,128)(2,1)S(1)}, u32[]{:S(2)}, u32[]{:S(2)}) %collective-permute-start.34) | collective-permute-done | bytes 540704 | tf_op jit(solution)/shard_map/ppermute | solution.py:49
  169.5 1.8 collective-permute-start.39
  171.6 1.0 collective-permute-start.40
  172.6 1.8 out_project.3
  174.4 8.7 %collective-permute-done.40.refs_2_ = bf16[512,512]{1,0:T(8,128)(2,1)S(1)} collective-permute-done((bf16[512,512]{1,0:T(8,128)(2,1)S(1)}, bf16[512,512]{1,0:T(8,128)(2,1)S(1)}, u32[]{:S(2)}, u32[]{:S(2)}) %collective-permute-start.40) | collective-permute-done | bytes 524320 | tf_op jit(solution)/shard_map/ppermute | solution.py:49
  183.1 1.4 collective-permute-done.38.refs_0_
  184.5 1.1 collective-permute-start.42
  186.2 1.6 out_project.4
  187.7 4.4 %collective-permute-done.41.refs_0_ = bf16[256,512]{1,0:T(8,128)(2,1)S(1)} collective-permute-done((bf16[256,512]{1,0:T(8,128)(2,1)S(1)}, bf16[256,512]{1,0:T(8,128)(2,1)S(1)}, u32[]{:S(2)}, u32[]{:S(2)}) %collective-permute-start.41) | collective-permute-done | bytes 262176 | tf_op jit(solution)/shard_map/ppermute | solution.py:49
  192.1 1.0 out_project.5
  193.1 4.7 %collective-permute-start.43 = (f32[528,256]{1,0:T(8,128)S(1)}, f32[528,256]{1,0:T(8,128)S(1)}, u32[]{:S(2)}, u32[]{:S(2)}) collective-permute-start(f32[528,256]{1,0:T(8,128)S(1)} %get-tuple-element.127), channel_id=1, source_target_pairs={{0,1},{1,0},{2,3},{3,2},{4,5},{5,4},{6,7},{7,6},{8,9},{9,8},{10,11... | collective-permute-start | bytes 1622024 | tf_op jit(solution)/shard_map/ppermute | solution.py:49
  197.8 1.6 collective-permute-done.43
  199.6 1.0 copy.35
  (133 shorter events, 9.5 us)
Async XLA Ops:
  1.7 6.8 %copy-start = (bf16[4096,256]{1,0:T(8,128)(2,1)S(1)}, bf16[4096,256]{1,0:T(8,128)(2,1)}, u32[]{:S(2)}) copy-start(bf16[4096,256]{1,0:T(8,128)(2,1)} %refs_2_.1) | copy-start | bytes 6291460
  2.7 1.9 collective-permute-start
  4.7 17.6 %copy-start.11 = (bf16[528,512]{1,0:T(8,128)(2,1)}, bf16[528,512]{1,0:T(8,128)(2,1)S(1)}, u32[]{:S(2)}) copy-start(bf16[528,512]{1,0:T(8,128)(2,1)S(1)} %pad_maximum_fusion.3.refs_0_) | copy-start | bytes 1622020
  4.7 14.9 %collective-permute-start.1 = (bf16[528,512]{1,0:T(8,128)(2,1)S(1)}, bf16[528,512]{1,0:T(8,128)(2,1)S(1)}, u32[]{:S(2)}, u32[]{:S(2)}) collective-permute-start(bf16[528,512]{1,0:T(8,128)(2,1)S(1)} %pad_maximum_fusion.3.refs_0_), channel_id=1, source_target_pairs={{0,2},{1,3},{2,4},{3,5},{4,6},{5,7},{6,0},{7,1},{8,10},{9,11},{10,... | collective-permute-start | bytes 1622024 | tf_op jit(solution)/shard_map/ppermute | solution.py:49
  6.1 13.5 %collective-permute-start.2 = (bf16[528,512]{1,0:T(8,128)(2,1)S(1)}, bf16[528,512]{1,0:T(8,128)(2,1)S(1)}, u32[]{:S(2)}, u32[]{:S(2)}) collective-permute-start(bf16[528,512]{1,0:T(8,128)(2,1)S(1)} %pad_maximum_fusion.3.refs_0_), channel_id=1, source_target_pairs={{0,6},{1,7},{2,0},{3,1},{4,2},{5,3},{6,4},{7,5},{8,14},{9,15},{10,... | collective-permute-start | bytes 1622024 | tf_op jit(solution)/shard_map/ppermute | solution.py:49
  7.6 13.0 %collective-permute-start.3 = (bf16[528,512]{1,0:T(8,128)(2,1)S(1)}, bf16[528,512]{1,0:T(8,128)(2,1)S(1)}, u32[]{:S(2)}, u32[]{:S(2)}) collective-permute-start(bf16[528,512]{1,0:T(8,128)(2,1)S(1)} %pad_maximum_fusion.3.refs_0_), channel_id=1, source_target_pairs={{0,8},{1,9},{2,10},{3,11},{4,12},{5,13},{6,14},{7,15},{8,0},{9,1},... | collective-permute-start | bytes 1622024 | tf_op jit(solution)/shard_map/ppermute | solution.py:49
  8.5 17.9 %collective-permute-start.4 = (bf16[4096,256]{1,0:T(8,128)(2,1)S(1)}, bf16[4096,256]{1,0:T(8,128)(2,1)S(1)}, u32[]{:S(2)}, u32[]{:S(2)}) collective-permute-start(bf16[4096,256]{1,0:T(8,128)(2,1)S(1)} %copy-done), channel_id=1, source_target_pairs={{0,1},{1,0},{2,3},{3,2},{4,5},{5,4},{6,7},{7,6},{8,9},{9,8},{10,11... | collective-permute-start | bytes 6291464 | tf_op jit(solution)/shard_map/ppermute | solution.py:49
  9.6 19.8 %collective-permute-start.5 = (bf16[4096,256]{1,0:T(8,128)(2,1)}, bf16[4096,256]{1,0:T(8,128)(2,1)}, u32[]{:S(2)}, u32[]{:S(2)}) collective-permute-start(bf16[4096,256]{1,0:T(8,128)(2,1)} %refs_3_.3), channel_id=1, source_target_pairs={{0,1},{1,0},{2,3},{3,2},{4,5},{5,4},{6,7},{7,6},{8,9},{9,8},{10,11... | collective-permute-start | bytes 6291464 | tf_op jit(solution)/shard_map/ppermute | solution.py:49
  19.6 5.0 %copy-start.14 = (bf16[528,512]{1,0:T(8,128)(2,1)}, bf16[528,512]{1,0:T(8,128)(2,1)S(1)}, u32[]{:S(2)}) copy-start(bf16[528,512]{1,0:T(8,128)(2,1)S(1)} %collective-permute-done.1.refs_1_) | copy-start | bytes 1622020
  19.6 3.6 %copy-start.12 = (bf16[528,512]{1,0:T(8,128)(2,1)}, bf16[528,512]{1,0:T(8,128)(2,1)S(1)}, u32[]{:S(2)}) copy-start(bf16[528,512]{1,0:T(8,128)(2,1)S(1)} %collective-permute-done.2.refs_2_) | copy-start | bytes 1622020
  20.6 1.7 copy-start.13
  20.6 8.8 %collective-permute-start.6 = (bf16[4096,256]{1,0:T(8,128)(2,1)}, bf16[4096,256]{1,0:T(8,128)(2,1)}, u32[]{:S(2)}, u32[]{:S(2)}) collective-permute-start(bf16[4096,256]{1,0:T(8,128)(2,1)} %refs_4_.5), channel_id=1, source_target_pairs={{0,1},{1,0},{2,3},{3,2},{4,5},{5,4},{6,7},{7,6},{8,9},{9,8},{10,11... | collective-permute-start | bytes 6291464 | tf_op jit(solution)/shard_map/ppermute | solution.py:49
  23.2 16.9 %collective-permute-start.8 = (bf16[544,512]{1,0:T(8,128)(2,1)}, bf16[544,512]{1,0:T(8,128)(2,1)S(1)}, u32[]{:S(2)}, u32[]{:S(2)}) collective-permute-start(bf16[544,512]{1,0:T(8,128)(2,1)} %pad_maximum_fusion.1), channel_id=1, source_target_pairs={{0,6},{1,7},{2,0},{3,1},{4,2},{5,3},{6,4},{7,5},{8,14},{9,15},{10,... | collective-permute-start | bytes 1671176 | tf_op jit(solution)/shard_map/ppermute | solution.py:49
  24.6 1.0 slice-start
  25.5 14.6 %collective-permute-start.7 = (bf16[528,512]{1,0:T(8,128)(2,1)}, bf16[528,512]{1,0:T(8,128)(2,1)S(1)}, u32[]{:S(2)}, u32[]{:S(2)}) collective-permute-start(bf16[528,512]{1,0:T(8,128)(2,1)} %pad_maximum_fusion.4), channel_id=1, source_target_pairs={{0,2},{1,3},{2,4},{3,5},{4,6},{5,7},{6,0},{7,1},{8,10},{9,11},{10,... | collective-permute-start | bytes 1622024 | tf_op jit(solution)/shard_map/ppermute | solution.py:49
  26.4 1.3 copy-start.4
  27.7 12.3 %collective-permute-start.9 = (bf16[512,512]{1,0:T(8,128)(2,1)}, bf16[512,512]{1,0:T(8,128)(2,1)S(1)}, u32[]{:S(2)}, u32[]{:S(2)}) collective-permute-start(bf16[512,512]{1,0:T(8,128)(2,1)} %pad_maximum_fusion.6), channel_id=1, source_target_pairs={{0,8},{1,9},{2,10},{3,11},{4,12},{5,13},{6,14},{7,15},{8,0},{9,1},... | collective-permute-start | bytes 1572872 | tf_op jit(solution)/shard_map/ppermute | solution.py:49
  29.3 13.5 %copy-start.7 = (s32[8]{0:T(128)S(1)}, s32[8]{0:T(128)}, u32[]{:S(2)}) copy-start(s32[8]{0:T(128)} %stack.57.idx) | copy-start | bytes 100
  29.3 13.5 %copy-start.1 = (bf16[4096,256]{1,0:T(8,128)(2,1)S(1)}, bf16[4096,256]{1,0:T(8,128)(2,1)}, u32[]{:S(2)}) copy-start(bf16[4096,256]{1,0:T(8,128)(2,1)} %refs_2_.1) | copy-start | bytes 6291460
  29.4 13.5 %copy-start.2 = (bf16[4096,256]{1,0:T(8,128)(2,1)S(1)}, bf16[4096,256]{1,0:T(8,128)(2,1)}, u32[]{:S(2)}) copy-start(bf16[4096,256]{1,0:T(8,128)(2,1)} %refs_3_.3) | copy-start | bytes 6291460
  29.4 13.5 %copy-start.3 = (bf16[4096,256]{1,0:T(8,128)(2,1)S(1)}, bf16[4096,256]{1,0:T(8,128)(2,1)}, u32[]{:S(2)}) copy-start(bf16[4096,256]{1,0:T(8,128)(2,1)} %refs_4_.5) | copy-start | bytes 6291460
  40.1 12.1 %collective-permute-start.11 = (bf16[272,512]{1,0:T(8,128)(2,1)S(1)}, bf16[272,512]{1,0:T(8,128)(2,1)S(1)}, u32[]{:S(2)}, u32[]{:S(2)}) collective-permute-start(bf16[272,512]{1,0:T(8,128)(2,1)S(1)} %slice.136), channel_id=1, source_target_pairs={{0,6},{1,7},{2,0},{3,1},{4,2},{5,3},{6,4},{7,5},{8,14},{9,15},{10,... | collective-permute-start | bytes 835592 | tf_op jit(solution)/shard_map/ppermute | solution.py:49
  42.7 9.5 %collective-permute-start.10 = (bf16[256,512]{1,0:T(8,128)(2,1)S(1)}, bf16[256,512]{1,0:T(8,128)(2,1)S(1)}, u32[]{:S(2)}, u32[]{:S(2)}) collective-permute-start(bf16[256,512]{1,0:T(8,128)(2,1)S(1)} %slice.135), channel_id=1, source_target_pairs={{0,2},{1,3},{2,4},{3,5},{4,6},{5,7},{6,0},{7,1},{8,10},{9,11},{10,... | collective-permute-start | bytes 786440 | tf_op jit(solution)/shard_map/ppermute | solution.py:49
  42.8 1.6 copy-start.5
  44.4 20.4 %copy-start.15 = (s32[128,4]{0,1:T(4,128)S(1)}, s32[128,4]{0,1:T(4,128)}, u32[]{:S(2)}) copy-start(s32[128,4]{0,1:T(4,128)} %param.20) | copy-start | bytes 6148
  44.4 36.9 %copy-start.16 = (s32[128]{0:T(128)S(1)}, s32[128]{0:T(128)}, u32[]{:S(2)}) copy-start(s32[128]{0:T(128)} %param.21) | copy-start | bytes 1540
  52.2 1.9 copy-start.6
  58.9 0.9 copy-start.9
  59.8 11.3 %collective-permute-start.12 = (bf16[544,384]{1,0:T(8,128)(2,1)}, bf16[544,384]{1,0:T(8,128)(2,1)S(1)}, u32[]{:S(2)}, u32[]{:S(2)}) collective-permute-start(bf16[544,384]{1,0:T(8,128)(2,1)} %get-tuple-element.76), channel_id=1, source_target_pairs={{0,16},{1,17},{2,18},{3,19},{4,20},{5,21},{6,22},{7,23},{8,24},{9,... | collective-permute-start | bytes 1253384 | tf_op jit(solution)/shard_map/ppermute | solution.py:49
  61.4 9.7 %collective-permute-start.13 = (bf16[544,384]{1,0:T(8,128)(2,1)}, bf16[544,384]{1,0:T(8,128)(2,1)S(1)}, u32[]{:S(2)}, u32[]{:S(2)}) collective-permute-start(bf16[544,384]{1,0:T(8,128)(2,1)} %get-tuple-element.77), channel_id=1, source_target_pairs={{0,48},{1,49},{2,50},{3,51},{4,52},{5,53},{6,54},{7,55},{8,56},{9,... | collective-permute-start | bytes 1253384 | tf_op jit(solution)/shard_map/ppermute | solution.py:49
  63.5 17.4 %collective-permute-start.14 = (bf16[544,384]{1,0:T(8,128)(2,1)S(1)}, bf16[544,384]{1,0:T(8,128)(2,1)S(1)}, u32[]{:S(2)}, u32[]{:S(2)}) collective-permute-start(bf16[544,384]{1,0:T(8,128)(2,1)S(1)} %get-tuple-element.78), channel_id=1, source_target_pairs={{0,32},{1,33},{2,34},{3,35},{4,36},{5,37},{6,38},{7,39},{8,40},{9,... | collective-permute-start | bytes 1253384 | tf_op jit(solution)/shard_map/ppermute | solution.py:49
  81.0 6.3 %collective-permute-start.15 = (bf16[4,2,16,256]{3,2,1,0:T(8,128)(2,1)S(1)}, bf16[4,2,16,256]{3,2,1,0:T(8,128)(2,1)S(1)}, u32[]{:S(2)}, u32[]{:S(2)}) collective-permute-start(bf16[4,2,16,256]{3,2,1,0:T(8,128)(2,1)S(1)} %pad_maximum_fusion.17), channel_id=1, source_target_pairs={{0,64},{1,65},{2,66},{3,67},{4,68},{5,69},{6,70},{7,71},{8,72},{9,... | collective-permute-start | bytes 196616 | tf_op jit(solution)/shard_map/ppermute | solution.py:49
  82.0 5.2 %copy-start.10 = (bf16[528,768]{1,0:T(8,128)(2,1)S(1)}, bf16[528,768]{1,0:T(8,128)(2,1)}, u32[]{:S(2)}) copy-start(bf16[528,768]{1,0:T(8,128)(2,1)} %copy-done.9) | copy-start | bytes 2433028
  82.1 25.4 %collective-permute-start.18 = (bf16[2048,256]{1,0:T(8,128)(2,1)S(1)}, bf16[2048,256]{1,0:T(8,128)(2,1)S(1)}, u32[]{:S(2)}, u32[]{:S(2)}) collective-permute-start(bf16[2048,256]{1,0:T(8,128)(2,1)S(1)} %pack.1.mine), channel_id=1, source_target_pairs={{0,1},{1,0},{2,3},{3,2},{4,5},{5,4},{6,7},{7,6},{8,9},{9,8},{10,11... | collective-permute-start | bytes 3145736 | tf_op jit(solution)/shard_map/ppermute | solution.py:49
  86.0 37.7 %collective-permute-start.23 = (bf16[2048,256]{1,0:T(8,128)(2,1)S(1)}, bf16[2048,256]{1,0:T(8,128)(2,1)S(1)}, u32[]{:S(2)}, u32[]{:S(2)}) collective-permute-start(bf16[2048,256]{1,0:T(8,128)(2,1)S(1)} %pack.1.mine), channel_id=1, source_target_pairs={{0,64},{1,65},{2,66},{3,67},{4,68},{5,69},{6,70},{7,71},{8,72},{9,... | collective-permute-start | bytes 3145736 | tf_op jit(solution)/shard_map/ppermute | solution.py:49
  87.3 9.9 %collective-permute-start.17 = (bf16[528,768]{1,0:T(8,128)(2,1)S(1)}, bf16[528,768]{1,0:T(8,128)(2,1)S(1)}, u32[]{:S(2)}, u32[]{:S(2)}) collective-permute-start(bf16[528,768]{1,0:T(8,128)(2,1)S(1)} %copy-done.10), channel_id=1, source_target_pairs={{0,1},{1,0},{2,3},{3,2},{4,5},{5,4},{6,7},{7,6},{8,9},{9,8},{10,11... | collective-permute-start | bytes 2433032 | tf_op jit(solution)/shard_map/ppermute | solution.py:49
  92.1 26.7 %collective-permute-start.21 = (bf16[256,1024]{1,0:T(8,128)(2,1)S(1)}, bf16[256,1024]{1,0:T(8,128)(2,1)S(1)}, u32[]{:S(2)}, u32[]{:S(2)}) collective-permute-start(bf16[256,1024]{1,0:T(8,128)(2,1)S(1)} %pad_maximum_fusion.10), channel_id=1, source_target_pairs={{0,6},{1,7},{2,0},{3,1},{4,2},{5,3},{6,4},{7,5},{8,14},{9,15},{10,... | collective-permute-start | bytes 1572872 | tf_op jit(solution)/shard_map/ppermute | solution.py:49
  94.8 2.2 %collective-permute-start.16 = (bf16[8,16,256]{2,1,0:T(8,128)(2,1)S(1)}, bf16[8,16,256]{2,1,0:T(8,128)(2,1)S(1)}, u32[]{:S(2)}, u32[]{:S(2)}) collective-permute-start(bf16[8,16,256]{2,1,0:T(8,128)(2,1)S(1)} %slice_bitcast_fusion.4), channel_id=1, source_target_pairs={{0,1},{1,0},{2,3},{3,2},{4,5},{5,4},{6,7},{7,6},{8,9},{9,8},{10,11... | collective-permute-start | bytes 196616 | tf_op jit(solution)/shard_map/ppermute | solution.py:49
  96.1 1.4 copy-start.8
  97.1 21.7 %collective-permute-start.20 = (bf16[256,1024]{1,0:T(8,128)(2,1)}, bf16[256,1024]{1,0:T(8,128)(2,1)S(1)}, u32[]{:S(2)}, u32[]{:S(2)}) collective-permute-start(bf16[256,1024]{1,0:T(8,128)(2,1)} %pad_maximum_fusion.9), channel_id=1, source_target_pairs={{0,4},{1,5},{2,6},{3,7},{4,0},{5,1},{6,2},{7,3},{8,12},{9,13},{10,... | collective-permute-start | bytes 1572872 | tf_op jit(solution)/shard_map/ppermute | solution.py:49
  97.2 26.4 %collective-permute-start.19 = (bf16[256,1024]{1,0:T(8,128)(2,1)}, bf16[256,1024]{1,0:T(8,128)(2,1)S(1)}, u32[]{:S(2)}, u32[]{:S(2)}) collective-permute-start(bf16[256,1024]{1,0:T(8,128)(2,1)} %pad_maximum_fusion.8), channel_id=1, source_target_pairs={{0,2},{1,3},{2,4},{3,5},{4,6},{5,7},{6,0},{7,1},{8,10},{9,11},{10,... | collective-permute-start | bytes 1572872 | tf_op jit(solution)/shard_map/ppermute | solution.py:49
  107.5 16.2 %collective-permute-start.22 = (f32[4,32,384]{2,1,0:T(8,128)S(1)}, f32[4,32,384]{2,1,0:T(8,128)S(1)}, u32[]{:S(2)}, u32[]{:S(2)}) collective-permute-start(f32[4,32,384]{2,1,0:T(8,128)S(1)} %slice.174), channel_id=1, source_target_pairs={{0,64},{1,65},{2,66},{3,67},{4,68},{5,69},{6,70},{7,71},{8,72},{9,... | collective-permute-start | bytes 589832 | tf_op jit(solution)/shard_map/ppermute | solution.py:49
  123.7 4.5 %collective-permute-start.24 = (bf16[2048,256]{1,0:T(8,128)(2,1)S(1)}, bf16[2048,256]{1,0:T(8,128)(2,1)S(1)}, u32[]{:S(2)}, u32[]{:S(2)}) collective-permute-start(bf16[2048,256]{1,0:T(8,128)(2,1)S(1)} %collective-permute-done.23.refs_3_.refs_1_), channel_id=1, source_target_pairs={{0,1},{1,0},{2,3},{3,2},{4,5},{5,4},{6,7},{7,6},{8,9},{9,8},{10,11... | collective-permute-start | bytes 3145736 | tf_op jit(solution)/shard_map/ppermute | solution.py:49
  124.5 16.1 %collective-permute-start.25 = (f32[2,32,384]{2,1,0:T(8,128)S(1)}, f32[2,32,384]{2,1,0:T(8,128)S(1)}, u32[]{:S(2)}, u32[]{:S(2)}) collective-permute-start(f32[2,32,384]{2,1,0:T(8,128)S(1)} %get-tuple-element.148), channel_id=1, source_target_pairs={{0,48},{1,49},{2,50},{3,51},{4,52},{5,53},{6,54},{7,55},{8,56},{9,... | collective-permute-start | bytes 294920 | tf_op jit(solution)/shard_map/ppermute | solution.py:49
  126.1 14.6 %collective-permute-start.26 = (f32[2,32,384]{2,1,0:T(8,128)S(1)}, f32[2,32,384]{2,1,0:T(8,128)S(1)}, u32[]{:S(2)}, u32[]{:S(2)}) collective-permute-start(f32[2,32,384]{2,1,0:T(8,128)S(1)} %get-tuple-element.150), channel_id=1, source_target_pairs={{0,32},{1,33},{2,34},{3,35},{4,36},{5,37},{6,38},{7,39},{8,40},{9,... | collective-permute-start | bytes 294920 | tf_op jit(solution)/shard_map/ppermute | solution.py:49
  127.3 13.4 %collective-permute-start.27 = (f32[2,32,384]{2,1,0:T(8,128)S(1)}, f32[2,32,384]{2,1,0:T(8,128)S(1)}, u32[]{:S(2)}, u32[]{:S(2)}) collective-permute-start(f32[2,32,384]{2,1,0:T(8,128)S(1)} %get-tuple-element.149), channel_id=1, source_target_pairs={{0,16},{1,17},{2,18},{3,19},{4,20},{5,21},{6,22},{7,23},{8,24},{9,... | collective-permute-start | bytes 294920 | tf_op jit(solution)/shard_map/ppermute | solution.py:49
  127.3 30.6 %collective-permute-start.36 = (bf16[1024,512]{1,0:T(8,128)(2,1)S(1)}, bf16[1024,512]{1,0:T(8,128)(2,1)S(1)}, u32[]{:S(2)}, u32[]{:S(2)}) collective-permute-start(bf16[1024,512]{1,0:T(8,128)(2,1)S(1)} %get-tuple-element.116), channel_id=1, source_target_pairs={{0,8},{1,9},{2,10},{3,11},{4,12},{5,13},{6,14},{7,15},{8,0},{9,1},... | collective-permute-start | bytes 3145736 | tf_op jit(solution)/shard_map/ppermute | solution.py:49
  141.4 9.9 %collective-permute-start.31 = (bf16[16,256]{1,0:T(8,128)(2,1)S(1)}, bf16[16,256]{1,0:T(8,128)(2,1)S(1)}, u32[]{:S(2)}, u32[]{:S(2)}) collective-permute-start(bf16[16,256]{1,0:T(8,128)(2,1)S(1)} %slice_select_fusion), channel_id=1, source_target_pairs={{0,1},{1,0},{2,3},{3,2},{4,5},{5,4},{6,7},{7,6},{8,9},{9,8},{10,11... | collective-permute-start | bytes 24584 | tf_op jit(solution)/shard_map/ppermute | solution.py:49
  142.4 8.9 %collective-permute-start.28 = (bf16[512,128]{1,0:T(8,128)(2,1)S(1)}, bf16[512,128]{1,0:T(8,128)(2,1)S(1)}, u32[]{:S(2)}, u32[]{:S(2)}) collective-permute-start(bf16[512,128]{1,0:T(8,128)(2,1)S(1)} %get-tuple-element.146), channel_id=1, source_target_pairs={{0,48},{1,49},{2,50},{3,51},{4,52},{5,53},{6,54},{7,55},{8,56},{9,... | collective-permute-start | bytes 393224 | tf_op jit(solution)/shard_map/ppermute | solution.py:49
  145.4 6.3 %collective-permute-start.29 = (bf16[512,128]{1,0:T(8,128)(2,1)S(1)}, bf16[512,128]{1,0:T(8,128)(2,1)S(1)}, u32[]{:S(2)}, u32[]{:S(2)}) collective-permute-start(bf16[512,128]{1,0:T(8,128)(2,1)S(1)} %get-tuple-element.145), channel_id=1, source_target_pairs={{0,32},{1,33},{2,34},{3,35},{4,36},{5,37},{6,38},{7,39},{8,40},{9,... | collective-permute-start | bytes 393224 | tf_op jit(solution)/shard_map/ppermute | solution.py:49
  146.0 9.1 %collective-permute-start.30 = (bf16[512,128]{1,0:T(8,128)(2,1)S(1)}, bf16[512,128]{1,0:T(8,128)(2,1)S(1)}, u32[]{:S(2)}, u32[]{:S(2)}) collective-permute-start(bf16[512,128]{1,0:T(8,128)(2,1)S(1)} %get-tuple-element.144), channel_id=1, source_target_pairs={{0,16},{1,17},{2,18},{3,19},{4,20},{5,21},{6,22},{7,23},{8,24},{9,... | collective-permute-start | bytes 393224 | tf_op jit(solution)/shard_map/ppermute | solution.py:49
  155.8 13.4 %collective-permute-start.34 = (bf16[528,512]{1,0:T(8,128)(2,1)S(1)}, bf16[528,512]{1,0:T(8,128)(2,1)S(1)}, u32[]{:S(2)}, u32[]{:S(2)}) collective-permute-start(bf16[528,512]{1,0:T(8,128)(2,1)S(1)} %head_order.1.refs_0_), channel_id=1, source_target_pairs={{0,8},{1,9},{2,10},{3,11},{4,12},{5,13},{6,14},{7,15},{8,0},{9,1},... | collective-permute-start | bytes 1622024 | tf_op jit(solution)/shard_map/ppermute | solution.py:49
  156.4 13.0 %collective-permute-start.33 = (bf16[528,512]{1,0:T(8,128)(2,1)S(1)}, bf16[528,512]{1,0:T(8,128)(2,1)S(1)}, u32[]{:S(2)}, u32[]{:S(2)}) collective-permute-start(bf16[528,512]{1,0:T(8,128)(2,1)S(1)} %head_order.1.refs_0_), channel_id=1, source_target_pairs={{0,6},{1,7},{2,0},{3,1},{4,2},{5,3},{6,4},{7,5},{8,14},{9,15},{10,... | collective-permute-start | bytes 1622024 | tf_op jit(solution)/shard_map/ppermute | solution.py:49
  157.0 14.4 %collective-permute-start.32 = (bf16[528,512]{1,0:T(8,128)(2,1)S(1)}, bf16[528,512]{1,0:T(8,128)(2,1)S(1)}, u32[]{:S(2)}, u32[]{:S(2)}) collective-permute-start(bf16[528,512]{1,0:T(8,128)(2,1)S(1)} %head_order.1.refs_0_), channel_id=1, source_target_pairs={{0,2},{1,3},{2,4},{3,5},{4,6},{5,7},{6,0},{7,1},{8,10},{9,11},{10,... | collective-permute-start | bytes 1622024 | tf_op jit(solution)/shard_map/ppermute | solution.py:49
  157.9 14.7 %collective-permute-start.37 = (bf16[1024,512]{1,0:T(8,128)(2,1)S(1)}, bf16[1024,512]{1,0:T(8,128)(2,1)S(1)}, u32[]{:S(2)}, u32[]{:S(2)}) collective-permute-start(bf16[1024,512]{1,0:T(8,128)(2,1)S(1)} %collective-permute-done.36.refs_6_.refs_5_.refs_4_), channel_id=1, source_target_pairs={{0,1},{1,0},{2,3},{3,2},{4,5},{5,4},{6,7},{7,6},{8,9},{9,8},{10,11... | collective-permute-start | bytes 3145736 | tf_op jit(solution)/shard_map/ppermute | solution.py:49
  159.2 13.3 %collective-permute-start.35 = (bf16[1024,512]{1,0:T(8,128)(2,1)S(1)}, bf16[1024,512]{1,0:T(8,128)(2,1)S(1)}, u32[]{:S(2)}, u32[]{:S(2)}) collective-permute-start(bf16[1024,512]{1,0:T(8,128)(2,1)S(1)} %get-tuple-element.115.refs_4_.refs_3_.refs_2_), channel_id=1, source_target_pairs={{0,1},{1,0},{2,3},{3,2},{4,5},{5,4},{6,7},{7,6},{8,9},{9,8},{10,11... | collective-permute-start | bytes 3145736 | tf_op jit(solution)/shard_map/ppermute | solution.py:49
  169.5 15.0 %collective-permute-start.39 = (bf16[544,512]{1,0:T(8,128)(2,1)S(1)}, bf16[544,512]{1,0:T(8,128)(2,1)S(1)}, u32[]{:S(2)}, u32[]{:S(2)}) collective-permute-start(bf16[544,512]{1,0:T(8,128)(2,1)S(1)} %pad_maximum_fusion.2), channel_id=1, source_target_pairs={{0,6},{1,7},{2,0},{3,1},{4,2},{5,3},{6,4},{7,5},{8,14},{9,15},{10,... | collective-permute-start | bytes 1671176 | tf_op jit(solution)/shard_map/ppermute | solution.py:49
  171.4 13.1 %collective-permute-start.38 = (bf16[528,512]{1,0:T(8,128)(2,1)S(1)}, bf16[528,512]{1,0:T(8,128)(2,1)S(1)}, u32[]{:S(2)}, u32[]{:S(2)}) collective-permute-start(bf16[528,512]{1,0:T(8,128)(2,1)S(1)} %pad_maximum_fusion.5), channel_id=1, source_target_pairs={{0,2},{1,3},{2,4},{3,5},{4,6},{5,7},{6,0},{7,1},{8,10},{9,11},{10,... | collective-permute-start | bytes 1622024 | tf_op jit(solution)/shard_map/ppermute | solution.py:49
  171.6 11.6 %collective-permute-start.40 = (bf16[512,512]{1,0:T(8,128)(2,1)S(1)}, bf16[512,512]{1,0:T(8,128)(2,1)S(1)}, u32[]{:S(2)}, u32[]{:S(2)}) collective-permute-start(bf16[512,512]{1,0:T(8,128)(2,1)S(1)} %pad_maximum_fusion.11), channel_id=1, source_target_pairs={{0,8},{1,9},{2,10},{3,11},{4,12},{5,13},{6,14},{7,15},{8,0},{9,1},... | collective-permute-start | bytes 1572872 | tf_op jit(solution)/shard_map/ppermute | solution.py:49
  184.5 7.6 %collective-permute-start.42 = (bf16[272,512]{1,0:T(8,128)(2,1)S(1)}, bf16[272,512]{1,0:T(8,128)(2,1)S(1)}, u32[]{:S(2)}, u32[]{:S(2)}) collective-permute-start(bf16[272,512]{1,0:T(8,128)(2,1)S(1)} %slice.163), channel_id=1, source_target_pairs={{0,6},{1,7},{2,0},{3,1},{4,2},{5,3},{6,4},{7,5},{8,14},{9,15},{10,... | collective-permute-start | bytes 835592 | tf_op jit(solution)/shard_map/ppermute | solution.py:49
  185.6 6.5 %collective-permute-start.41 = (bf16[256,512]{1,0:T(8,128)(2,1)S(1)}, bf16[256,512]{1,0:T(8,128)(2,1)S(1)}, u32[]{:S(2)}, u32[]{:S(2)}) collective-permute-start(bf16[256,512]{1,0:T(8,128)(2,1)S(1)} %slice.162), channel_id=1, source_target_pairs={{0,2},{1,3},{2,4},{3,5},{4,6},{5,7},{6,0},{7,1},{8,10},{9,11},{10,... | collective-permute-start | bytes 786440 | tf_op jit(solution)/shard_map/ppermute | solution.py:49
  193.1 6.2 %collective-permute-start.43 = (f32[528,256]{1,0:T(8,128)S(1)}, f32[528,256]{1,0:T(8,128)S(1)}, u32[]{:S(2)}, u32[]{:S(2)}) collective-permute-start(f32[528,256]{1,0:T(8,128)S(1)} %get-tuple-element.127), channel_id=1, source_target_pairs={{0,1},{1,0},{2,3},{3,2},{4,5},{5,4},{6,7},{7,6},{8,9},{9,8},{10,11... | collective-permute-start | bytes 1622024 | tf_op jit(solution)/shard_map/ppermute | solution.py:49

commit v2 on v1

--- a/solution.py
+++ b/solution.py
@@ -138,33 +138,35 @@
 
         lax.fori_loop(0, 6, one, None)
         return
-    for n in range(6):
-        result = product(n)
-        y_ref, z_refs = refs[0], refs[1:5]
-        rel, kind = n // 3, n % 3
-        owner = core if rel == 0 else 1 - core
-        if kind == 0:
-            result = result * SCALE
-        result = result.astype(BF)
-        for head in range(2):
-            slot = lax.rem(owner * 2 + head - z + 4, 4)
+    y_ref, z_refs, sib_ref = refs[0], refs[1:5], refs[5]
+
+    def side(rel, _):
+        owner = jnp.where(rel == 0, core, 1 - core)
+        rows = pl.ds(pl.multiple_of(HALF + rel * DEC, DEC), DEC)
+        for kind in range(3):
+            result = product(rel * 3 + kind)
+            if kind == 0:
+                result = result * SCALE
+            result = result.astype(BF)
             for k in range(4):
-
-                @pl.when(slot == k)
+                for head in range(2):
+
+                    @pl.when(lax.rem(owner * 2 + head - z + 4, 4) == k)
+                    def _():
+                        z_refs[k][:HALF, kind * 128 : (kind + 1) * 128] = result[
+                            :HALF, head * 128 : (head + 1) * 128
+                        ]
+
+                if kind == 0:
+                    z_refs[k][rows, :256] = result[HALF:]
+                    z_refs[k][rows, 256:] = result[HALF:, :128]
+            for index, target in enumerate((y_ref, sib_ref)):
+
+                @pl.when(rel == index)
                 def _():
-                    z_refs[k][:HALF, kind * 128 : (kind + 1) * 128] = result[
-                        :HALF, head * 128 : (head + 1) * 128
-                    ]
-
-        if kind == 0:
-            rows = slice(HALF + rel * DEC, HALF + (rel + 1) * DEC)
-            for z_ref in z_refs:
-                z_ref[rows, :256] = result[HALF:]
-                z_ref[rows, 256:] = result[HALF:, :128]
-        if rel == 1:
-            refs[5][:, kind * 256 : (kind + 1) * 256] = result
-        else:
-            y_ref[:, kind * 256 : (kind + 1) * 256] = result
+                    target[:, kind * 256 : (kind + 1) * 256] = result
+
+    lax.fori_loop(0, 2, side, None)
 
 
 def vmem_spec():

time: 200 us -> 200 us (level); the launches traced: 201 us -> 199 us
    pallas_call x2, Pallas kernels: 17.7 us -> 14 us  [attend_cross(): pl.pallas_call(functools.partial(attend_cross_kernel, which), out_shape=j...]
    pallas_call x1, Pallas kernels: 9.82 us -> 12.1 us  [attend_own(): pl.pallas_call(attend_own_kernel, out_shape=(jax.ShapeDtypeStruct((4, HAL...]
  transfers between devices with their start and end apart: 44 -> 44, of which waited for: 15 -> 16; matrix products, arithmetic and copies ran while one was open for 4% -> 4% of each run, Pallas kernels for 30% -> 30%
where the time goes in v2:
time: 200 us; the launch traced here: 199 us
  Pallas kernels  64.3 us (32%)
  waiting for transfers between devices  62.5 us (31%)
  starting transfers between devices  52.5 us (26%)
  local copies, waits for them, and re-layouts  11.8 us (6%)
  other arithmetic  5.93 us (3%)
    ppermute x44, waiting for transfers between devices, move(): return lax.ppermute(x, AX, perm(**steps))  62.5 us
    ppermute x44, starting transfers between devices, move(): return lax.ppermute(x, AX, perm(**steps))  52.5 us
    pallas_call x3, Pallas kernels, qkv(): pl.pallas_call(functools.partial(qkv_kernel, step), out_shape=shape, in_s...  22.4 us
    pallas_call x2, Pallas kernels, attend_cross(): pl.pallas_call(functools.partial(attend_cross_kernel, which), out_shape=j...  14 us
    pallas_call x1, Pallas kernels, attend_own(): pl.pallas_call(attend_own_kernel, out_shape=(jax.ShapeDtypeStruct((4, HAL...  12.1 us
    pallas_call x1, Pallas kernels, decode_parts(): pl.pallas_call(decode_kernel, out_shape=jax.ShapeDtypeStruct((8, 32, 384)...  9.95 us
    unnamed x35, local copies, waits for them, and re-layouts  5.75 us
    pallas_call x3, Pallas kernels, out_project(): pl.pallas_call(functools.partial(out_kernel, step), out_shape=(jax.ShapeD...  4.38 us
  transfers between devices with their start and end apart: 44, of which 16 were waited for; matrix products, arithmetic and copies ran while one was open for 4% of the time, Pallas kernels for 30%

profile of v2, /device:TPU:5, one launch (start us, length us, event | category | flops | bytes accessed | tf_op | source)
XLA Modules:
  0.0 198.5 jit_solution(14349746132413479397)
XLA Ops:
  0.6 1.1 fusion.8
  1.7 0.9 slice_bitcast_fusion.9
  2.7 0.8 collective-permute-start
  3.5 1.2 collective-permute-done
  4.7 1.4 collective-permute-start.1
  6.1 1.5 collective-permute-start.2
  7.6 0.9 collective-permute-start.3
  8.5 1.1 collective-permute-start.4
  9.6 10.0 %collective-permute-done.1.refs_1_ = bf16[528,512]{1,0:T(8,128)(2,1)S(1)} collective-permute-done((bf16[528,512]{1,0:T(8,128)(2,1)S(1)}, bf16[528,512]{1,0:T(8,128)(2,1)S(1)}, u32[]{:S(2)}, u32[]{:S(2)}) %collective-permute-start.1) | collective-permute-done | bytes 540704 | tf_op jit(solution)/shard_map/ppermute | solution.py:49
  19.6 1.0 collective-permute-done.3.refs_3_
  20.6 1.7 collective-permute-start.6
  22.3 0.8 pad_maximum_fusion.1
  23.2 1.4 collective-permute-start.8
  24.6 0.9 pad_maximum_fusion.4
  25.6 0.9 pad_maximum_fusion.6
  26.4 1.3 copy-done.4
  27.7 0.9 collective-permute-start.9
  29.4 10.1 %qkv.3.refs_9_ = f32[6,528,256]{2,1,0:T(8,128)} custom-call(s32[8]{0:T(128)} %stack.57.idx, bf16[528,512]{1,0:T(8,128)(2,1)} %copy-done.11, bf16[528,512]{1,0:T(8,128)(2,1)} %copy-done.14, bf16[528,512]{1,0:T(8,128)(2,1)} %copy-done.12, bf16[528,512]{1,0:T(8,128)(2,1)} %copy-done.13, bf16[4096,256]{1,0:T(8,128)(2,1)} %refs_2_.1, bf16[4096,256]{1,0:T(8,128)(2,1)} %refs_3_.3, ...), custom_call_target="tpu_custom_call" | custom-call | flops 3321888768 | bytes 8388608 | tf_op jit(solution)/shard_map/qkv/pallas_call | solution.py:189
  40.1 2.6 %collective-permute-start.11 = (bf16[272,512]{1,0:T(8,128)(2,1)S(1)}, bf16[272,512]{1,0:T(8,128)(2,1)S(1)}, u32[]{:S(2)}, u32[]{:S(2)}) collective-permute-start(bf16[272,512]{1,0:T(8,128)(2,1)S(1)} %slice.136), channel_id=1, source_target_pairs={{0,6},{1,7},{2,0},{3,1},{4,2},{5,3},{6,4},{7,5},{8,14},{9,15},{10,... | collective-permute-start | bytes 835592 | tf_op jit(solution)/shard_map/ppermute | solution.py:49
  42.8 1.6 copy-done.5
  44.4 7.7 %qkv.4.refs_8_ = f32[6,528,256]{2,1,0:T(8,128)} custom-call(s32[8]{0:T(128)S(1)} %copy-done.7, bf16[528,512]{1,0:T(8,128)(2,1)S(1)} %collective-permute-done.7.refs_0_, bf16[544,512]{1,0:T(8,128)(2,1)S(1)} %collective-permute-done.8.refs_1_, bf16[512,512]{1,0:T(8,128)(2,1)S(1)} %collective-permute-done.9.refs_2_, bf16[4096,256]{1,0:T(8,128)(2,1)S(1)} %copy-done.1, ...), custom_call_target="tpu_custom_call" | custom-call | flops 2491416576 | bytes 8388608 | tf_op jit(solution)/shard_map/qkv/pallas_call | solution.py:189
  52.2 1.9 copy-done.6
  54.1 4.6 %qkv.5 = (bf16[528,768]{1,0:T(8,128)(2,1)S(1)}, bf16[544,384]{1,0:T(8,128)(2,1)S(1)}, bf16[544,384]{1,0:T(8,128)(2,1)}, bf16[544,384]{1,0:T(8,128)(2,1)S(1)}, bf...) custom-call(s32[8]{0:T(128)S(1)} %copy-done.7, bf16[256,512]{1,0:T(8,128)(2,1)S(1)} %collective-permute-done.10.refs_0_, ...), custom_call_target="tpu_custom_call" | custom-call | flops 830472192 | bytes 8388608 | tf_op jit(solution)/shard_map/qkv/pallas_call | solution.py:189
  58.7 0.9 copy-done.9
  59.6 1.6 collective-permute-start.12
  61.2 2.1 %collective-permute-start.13 = (bf16[544,384]{1,0:T(8,128)(2,1)}, bf16[544,384]{1,0:T(8,128)(2,1)S(1)}, u32[]{:S(2)}, u32[]{:S(2)}) collective-permute-start(bf16[544,384]{1,0:T(8,128)(2,1)} %get-tuple-element.77), channel_id=1, source_target_pairs={{0,48},{1,49},{2,50},{3,51},{4,52},{5,53},{6,54},{7,55},{8,56},{9,... | collective-permute-start | bytes 1253384 | tf_op jit(solution)/shard_map/ppermute | solution.py:49
  63.3 1.3 collective-permute-start.14
  64.8 6.2 %collective-permute-done.12.b.q1.refs_0_ = bf16[544,384]{1,0:T(8,128)(2,1)S(1)} collective-permute-done((bf16[544,384]{1,0:T(8,128)(2,1)}, bf16[544,384]{1,0:T(8,128)(2,1)S(1)}, u32[]{:S(2)}, u32[]{:S(2)}) %collective-permute-start.12) | collective-permute-done | bytes 417824 | tf_op jit(solution)/shard_map/ppermute | solution.py:49
  70.9 9.8 %collective-permute-done.14.c.q2.refs_1_ = bf16[544,384]{1,0:T(8,128)(2,1)S(1)} collective-permute-done((bf16[544,384]{1,0:T(8,128)(2,1)S(1)}, bf16[544,384]{1,0:T(8,128)(2,1)S(1)}, u32[]{:S(2)}, u32[]{:S(2)}) %collective-permute-start.14) | collective-permute-done | bytes 417824 | tf_op jit(solution)/shard_map/ppermute | solution.py:49
  81.9 3.9 %collective-permute-start.18 = (bf16[2048,256]{1,0:T(8,128)(2,1)S(1)}, bf16[2048,256]{1,0:T(8,128)(2,1)S(1)}, u32[]{:S(2)}, u32[]{:S(2)}) collective-permute-start(bf16[2048,256]{1,0:T(8,128)(2,1)S(1)} %pack.1.mine), channel_id=1, source_target_pairs={{0,1},{1,0},{2,3},{3,2},{4,5},{5,4},{6,7},{7,6},{8,9},{9,8},{10,11... | collective-permute-start | bytes 3145736 | tf_op jit(solution)/shard_map/ppermute | solution.py:49
  85.8 1.3 collective-permute-start.23
  87.1 3.1 %collective-permute-start.17 = (bf16[528,768]{1,0:T(8,128)(2,1)S(1)}, bf16[528,768]{1,0:T(8,128)(2,1)S(1)}, u32[]{:S(2)}, u32[]{:S(2)}) collective-permute-start(bf16[528,768]{1,0:T(8,128)(2,1)S(1)} %copy-done.10), channel_id=1, source_target_pairs={{0,1},{1,0},{2,3},{3,2},{4,5},{5,4},{6,7},{7,6},{8,9},{9,8},{10,11... | collective-permute-start | bytes 2433032 | tf_op jit(solution)/shard_map/ppermute | solution.py:49
  90.2 1.7 constant_dynamic-slice_fusion.1
  91.9 2.7 %collective-permute-start.21 = (bf16[256,1024]{1,0:T(8,128)(2,1)S(1)}, bf16[256,1024]{1,0:T(8,128)(2,1)S(1)}, u32[]{:S(2)}, u32[]{:S(2)}) collective-permute-start(bf16[256,1024]{1,0:T(8,128)(2,1)S(1)} %pad_maximum_fusion.10), channel_id=1, source_target_pairs={{0,6},{1,7},{2,0},{3,1},{4,2},{5,3},{6,4},{7,5},{8,14},{9,15},{10,... | collective-permute-start | bytes 1572872 | tf_op jit(solution)/shard_map/ppermute | solution.py:49
  95.0 0.9 pad_maximum_fusion.9
  95.9 0.9 pad_maximum_fusion.8
  97.5 9.9 %decode_parts.1 = f32[8,32,384]{2,1,0:T(8,128)S(1)} custom-call(s32[8]{0:T(128)S(1)} %copy-done.7, s32[8]{0:T(128)S(1)} %copy-done.8, bf16[256,256]{1,0:T(8,128)(2,1)S(1)} %bitcast.73, bf16[128,4,16,256]{3,2,1,0:T(8,128)(2,1)} %keys.1, bf16[128,4,16,256]{3,2,1,0:T(8,128)(2,1)} %values.1, f32[8,1024]{1,0:T(8,128)S(1)} %reshape.39.ok_ref, ...), custom_call_target="tpu_custom_call" | custom-call | flops 536870912 | bytes 10485760 | tf_op jit(solution)/shard_map/decode_parts/pallas_call | solution.py:515
  107.5 1.3 collective-permute-start.22
  108.8 12.1 %attend_own.1 = (f32[4,512,256]{2,1,0:T(8,128)S(1)}, f32[4,512,128]{2,1,0:T(8,128)S(1)}) custom-call(s32[8]{0:T(128)S(1)} %copy-done.7, s32[8]{0:T(128)S(1)} %copy-done.8, bf16[544,384]{1,0:T(8,128)(2,1)S(1)} %get-tuple-element.80.a.q0.refs_0_, bf16[544,384]{1,0:T(8,128)(2,1)S(1)} %collective-permute-done.12.b.q1.refs_0_, ...), custom_call_target="tpu_custom_call" | custom-call | flops 2147483648 | bytes 4194304 | tf_op jit(solution)/shard_map/attend_own/pallas_call | solution.py:353
  120.9 2.6 %collective-permute-done.19.b = bf16[256,1024]{1,0:T(8,128)(2,1)S(1)} collective-permute-done((bf16[256,1024]{1,0:T(8,128)(2,1)}, bf16[256,1024]{1,0:T(8,128)(2,1)S(1)}, u32[]{:S(2)}, u32[]{:S(2)}) %collective-permute-start.19) | collective-permute-done | bytes 524320 | tf_op jit(solution)/shard_map/ppermute | solution.py:49
  123.7 0.8 collective-permute-start.24
  124.5 1.6 collective-permute-start.25
  126.1 1.1 collective-permute-start.26
  127.2 0.9 collective-permute-start.36
  128.2 9.8 %attend_cross.2 = bf16[3,512,128]{2,1,0:T(8,128)(2,1)S(1)} custom-call(s32[8]{0:T(128)S(1)} %copy-done.7, s32[8]{0:T(128)S(1)} %copy-done.8, bf16[544,384]{1,0:T(8,128)(2,1)S(1)} %collective-permute-done.12.b.q1.refs_0_, bf16[544,384]{1,0:T(8,128)(2,1)S(1)} %collective-permute-done.14.c.q2.refs_1_, ...), custom_call_target="tpu_custom_call" | custom-call | flops 2147483648 | bytes 4194304 | tf_op jit(solution)/shard_map/attend_cross/pallas_call | solution.py:414
  138.6 0.9 collective-permute-start.31
  139.6 3.0 %collective-permute-start.28 = (bf16[512,128]{1,0:T(8,128)(2,1)S(1)}, bf16[512,128]{1,0:T(8,128)(2,1)S(1)}, u32[]{:S(2)}, u32[]{:S(2)}) collective-permute-start(bf16[512,128]{1,0:T(8,128)(2,1)S(1)} %get-tuple-element.146), channel_id=1, source_target_pairs={{0,48},{1,49},{2,50},{3,51},{4,52},{5,53},{6,54},{7,55},{8,56},{9,... | collective-permute-start | bytes 393224 | tf_op jit(solution)/shard_map/ppermute | solution.py:49
  143.3 4.2 %attend_cross.3 = bf16[1,512,128]{2,1,0:T(8,128)(2,1)S(1)} custom-call(s32[8]{0:T(128)S(1)} %copy-done.7, s32[8]{0:T(128)S(1)} %copy-done.8, bf16[544,384]{1,0:T(8,128)(2,1)S(1)} %get-tuple-element.80.a.q0.refs_0_, bf16[2048,256]{1,0:T(8,128)(2,1)S(1)} %collective-permute-done.23.refs_3_.refs_1_, ...), custom_call_target="tpu_custom_call" | custom-call | flops 2147483648 | bytes 4194304 | tf_op jit(solution)/shard_map/attend_cross/pallas_call | solution.py:414
  149.0 3.4 %collective-permute-done.30.d = bf16[512,128]{1,0:T(8,128)(2,1)S(1)} collective-permute-done((bf16[512,128]{1,0:T(8,128)(2,1)S(1)}, bf16[512,128]{1,0:T(8,128)(2,1)S(1)}, u32[]{:S(2)}, u32[]{:S(2)}) %collective-permute-start.30) | collective-permute-done | bytes 131104 | tf_op jit(solution)/shard_map/ppermute | solution.py:49
  154.2 0.9 collective-permute-start.32
  155.2 1.3 collective-permute-start.37
  156.5 10.0 %collective-permute-done.34.refs_3_ = bf16[528,512]{1,0:T(8,128)(2,1)S(1)} collective-permute-done((bf16[528,512]{1,0:T(8,128)(2,1)S(1)}, bf16[528,512]{1,0:T(8,128)(2,1)S(1)}, u32[]{:S(2)}, u32[]{:S(2)}) %collective-permute-start.34) | collective-permute-done | bytes 540704 | tf_op jit(solution)/shard_map/ppermute | solution.py:49
  166.8 1.8 collective-permute-start.39
  168.8 1.0 collective-permute-start.40
  169.8 1.8 out_project.3
  171.7 8.7 %collective-permute-done.40.refs_2_ = bf16[512,512]{1,0:T(8,128)(2,1)S(1)} collective-permute-done((bf16[512,512]{1,0:T(8,128)(2,1)S(1)}, bf16[512,512]{1,0:T(8,128)(2,1)S(1)}, u32[]{:S(2)}, u32[]{:S(2)}) %collective-permute-start.40) | collective-permute-done | bytes 524320 | tf_op jit(solution)/shard_map/ppermute | solution.py:49
  180.4 1.4 collective-permute-done.38.refs_0_
  181.8 1.1 collective-permute-start.42
  183.4 1.6 out_project.4
  185.0 4.4 %collective-permute-done.41.refs_0_ = bf16[256,512]{1,0:T(8,128)(2,1)S(1)} collective-permute-done((bf16[256,512]{1,0:T(8,128)(2,1)S(1)}, bf16[256,512]{1,0:T(8,128)(2,1)S(1)}, u32[]{:S(2)}, u32[]{:S(2)}) %collective-permute-start.41) | collective-permute-done | bytes 262176 | tf_op jit(solution)/shard_map/ppermute | solution.py:49
  189.4 1.0 out_project.5
  190.4 4.7 %collective-permute-start.43 = (f32[528,256]{1,0:T(8,128)S(1)}, f32[528,256]{1,0:T(8,128)S(1)}, u32[]{:S(2)}, u32[]{:S(2)}) collective-permute-start(f32[528,256]{1,0:T(8,128)S(1)} %get-tuple-element.127), channel_id=1, source_target_pairs={{0,1},{1,0},{2,3},{3,2},{4,5},{5,4},{6,7},{7,6},{8,9},{9,8},{10,11... | collective-permute-start | bytes 1622024 | tf_op jit(solution)/shard_map/ppermute | solution.py:49
  195.0 1.6 collective-permute-done.43
  196.9 1.0 copy.35
  (133 shorter events, 10.7 us)
Async XLA Ops:
  1.7 6.8 %copy-start = (bf16[4096,256]{1,0:T(8,128)(2,1)S(1)}, bf16[4096,256]{1,0:T(8,128)(2,1)}, u32[]{:S(2)}) copy-start(bf16[4096,256]{1,0:T(8,128)(2,1)} %refs_2_.1) | copy-start | bytes 6291460
  2.7 1.9 collective-permute-start
  4.7 17.6 %copy-start.11 = (bf16[528,512]{1,0:T(8,128)(2,1)}, bf16[528,512]{1,0:T(8,128)(2,1)S(1)}, u32[]{:S(2)}) copy-start(bf16[528,512]{1,0:T(8,128)(2,1)S(1)} %pad_maximum_fusion.3.refs_0_) | copy-start | bytes 1622020
  4.7 14.9 %collective-permute-start.1 = (bf16[528,512]{1,0:T(8,128)(2,1)S(1)}, bf16[528,512]{1,0:T(8,128)(2,1)S(1)}, u32[]{:S(2)}, u32[]{:S(2)}) collective-permute-start(bf16[528,512]{1,0:T(8,128)(2,1)S(1)} %pad_maximum_fusion.3.refs_0_), channel_id=1, source_target_pairs={{0,2},{1,3},{2,4},{3,5},{4,6},{5,7},{6,0},{7,1},{8,10},{9,11},{10,... | collective-permute-start | bytes 1622024 | tf_op jit(solution)/shard_map/ppermute | solution.py:49
  6.1 13.5 %collective-permute-start.2 = (bf16[528,512]{1,0:T(8,128)(2,1)S(1)}, bf16[528,512]{1,0:T(8,128)(2,1)S(1)}, u32[]{:S(2)}, u32[]{:S(2)}) collective-permute-start(bf16[528,512]{1,0:T(8,128)(2,1)S(1)} %pad_maximum_fusion.3.refs_0_), channel_id=1, source_target_pairs={{0,6},{1,7},{2,0},{3,1},{4,2},{5,3},{6,4},{7,5},{8,14},{9,15},{10,... | collective-permute-start | bytes 1622024 | tf_op jit(solution)/shard_map/ppermute | solution.py:49
  7.6 13.0 %collective-permute-start.3 = (bf16[528,512]{1,0:T(8,128)(2,1)S(1)}, bf16[528,512]{1,0:T(8,128)(2,1)S(1)}, u32[]{:S(2)}, u32[]{:S(2)}) collective-permute-start(bf16[528,512]{1,0:T(8,128)(2,1)S(1)} %pad_maximum_fusion.3.refs_0_), channel_id=1, source_target_pairs={{0,8},{1,9},{2,10},{3,11},{4,12},{5,13},{6,14},{7,15},{8,0},{9,1},... | collective-permute-start | bytes 1622024 | tf_op jit(solution)/shard_map/ppermute | solution.py:49
  8.5 17.9 %collective-permute-start.4 = (bf16[4096,256]{1,0:T(8,128)(2,1)S(1)}, bf16[4096,256]{1,0:T(8,128)(2,1)S(1)}, u32[]{:S(2)}, u32[]{:S(2)}) collective-permute-start(bf16[4096,256]{1,0:T(8,128)(2,1)S(1)} %copy-done), channel_id=1, source_target_pairs={{0,1},{1,0},{2,3},{3,2},{4,5},{5,4},{6,7},{7,6},{8,9},{9,8},{10,11... | collective-permute-start | bytes 6291464 | tf_op jit(solution)/shard_map/ppermute | solution.py:49
  9.6 19.8 %collective-permute-start.5 = (bf16[4096,256]{1,0:T(8,128)(2,1)}, bf16[4096,256]{1,0:T(8,128)(2,1)}, u32[]{:S(2)}, u32[]{:S(2)}) collective-permute-start(bf16[4096,256]{1,0:T(8,128)(2,1)} %refs_3_.3), channel_id=1, source_target_pairs={{0,1},{1,0},{2,3},{3,2},{4,5},{5,4},{6,7},{7,6},{8,9},{9,8},{10,11... | collective-permute-start | bytes 6291464 | tf_op jit(solution)/shard_map/ppermute | solution.py:49
  19.6 5.0 %copy-start.14 = (bf16[528,512]{1,0:T(8,128)(2,1)}, bf16[528,512]{1,0:T(8,128)(2,1)S(1)}, u32[]{:S(2)}) copy-start(bf16[528,512]{1,0:T(8,128)(2,1)S(1)} %collective-permute-done.1.refs_1_) | copy-start | bytes 1622020
  19.6 3.6 %copy-start.12 = (bf16[528,512]{1,0:T(8,128)(2,1)}, bf16[528,512]{1,0:T(8,128)(2,1)S(1)}, u32[]{:S(2)}) copy-start(bf16[528,512]{1,0:T(8,128)(2,1)S(1)} %collective-permute-done.2.refs_2_) | copy-start | bytes 1622020
  20.6 1.7 copy-start.13
  20.6 8.8 %collective-permute-start.6 = (bf16[4096,256]{1,0:T(8,128)(2,1)}, bf16[4096,256]{1,0:T(8,128)(2,1)}, u32[]{:S(2)}, u32[]{:S(2)}) collective-permute-start(bf16[4096,256]{1,0:T(8,128)(2,1)} %refs_4_.5), channel_id=1, source_target_pairs={{0,1},{1,0},{2,3},{3,2},{4,5},{5,4},{6,7},{7,6},{8,9},{9,8},{10,11... | collective-permute-start | bytes 6291464 | tf_op jit(solution)/shard_map/ppermute | solution.py:49
  23.2 16.9 %collective-permute-start.8 = (bf16[544,512]{1,0:T(8,128)(2,1)}, bf16[544,512]{1,0:T(8,128)(2,1)S(1)}, u32[]{:S(2)}, u32[]{:S(2)}) collective-permute-start(bf16[544,512]{1,0:T(8,128)(2,1)} %pad_maximum_fusion.1), channel_id=1, source_target_pairs={{0,6},{1,7},{2,0},{3,1},{4,2},{5,3},{6,4},{7,5},{8,14},{9,15},{10,... | collective-permute-start | bytes 1671176 | tf_op jit(solution)/shard_map/ppermute | solution.py:49
  24.6 1.0 slice-start
  25.5 14.6 %collective-permute-start.7 = (bf16[528,512]{1,0:T(8,128)(2,1)}, bf16[528,512]{1,0:T(8,128)(2,1)S(1)}, u32[]{:S(2)}, u32[]{:S(2)}) collective-permute-start(bf16[528,512]{1,0:T(8,128)(2,1)} %pad_maximum_fusion.4), channel_id=1, source_target_pairs={{0,2},{1,3},{2,4},{3,5},{4,6},{5,7},{6,0},{7,1},{8,10},{9,11},{10,... | collective-permute-start | bytes 1622024 | tf_op jit(solution)/shard_map/ppermute | solution.py:49
  26.4 1.3 copy-start.4
  27.7 12.3 %collective-permute-start.9 = (bf16[512,512]{1,0:T(8,128)(2,1)}, bf16[512,512]{1,0:T(8,128)(2,1)S(1)}, u32[]{:S(2)}, u32[]{:S(2)}) collective-permute-start(bf16[512,512]{1,0:T(8,128)(2,1)} %pad_maximum_fusion.6), channel_id=1, source_target_pairs={{0,8},{1,9},{2,10},{3,11},{4,12},{5,13},{6,14},{7,15},{8,0},{9,1},... | collective-permute-start | bytes 1572872 | tf_op jit(solution)/shard_map/ppermute | solution.py:49
  29.3 13.5 %copy-start.7 = (s32[8]{0:T(128)S(1)}, s32[8]{0:T(128)}, u32[]{:S(2)}) copy-start(s32[8]{0:T(128)} %stack.57.idx) | copy-start | bytes 100
  29.3 13.5 %copy-start.1 = (bf16[4096,256]{1,0:T(8,128)(2,1)S(1)}, bf16[4096,256]{1,0:T(8,128)(2,1)}, u32[]{:S(2)}) copy-start(bf16[4096,256]{1,0:T(8,128)(2,1)} %refs_2_.1) | copy-start | bytes 6291460
  29.4 13.5 %copy-start.2 = (bf16[4096,256]{1,0:T(8,128)(2,1)S(1)}, bf16[4096,256]{1,0:T(8,128)(2,1)}, u32[]{:S(2)}) copy-start(bf16[4096,256]{1,0:T(8,128)(2,1)} %refs_3_.3) | copy-start | bytes 6291460
  29.4 13.5 %copy-start.3 = (bf16[4096,256]{1,0:T(8,128)(2,1)S(1)}, bf16[4096,256]{1,0:T(8,128)(2,1)}, u32[]{:S(2)}) copy-start(bf16[4096,256]{1,0:T(8,128)(2,1)} %refs_4_.5) | copy-start | bytes 6291460
  40.1 12.1 %collective-permute-start.11 = (bf16[272,512]{1,0:T(8,128)(2,1)S(1)}, bf16[272,512]{1,0:T(8,128)(2,1)S(1)}, u32[]{:S(2)}, u32[]{:S(2)}) collective-permute-start(bf16[272,512]{1,0:T(8,128)(2,1)S(1)} %slice.136), channel_id=1, source_target_pairs={{0,6},{1,7},{2,0},{3,1},{4,2},{5,3},{6,4},{7,5},{8,14},{9,15},{10,... | collective-permute-start | bytes 835592 | tf_op jit(solution)/shard_map/ppermute | solution.py:49
  42.7 9.5 %collective-permute-start.10 = (bf16[256,512]{1,0:T(8,128)(2,1)S(1)}, bf16[256,512]{1,0:T(8,128)(2,1)S(1)}, u32[]{:S(2)}, u32[]{:S(2)}) collective-permute-start(bf16[256,512]{1,0:T(8,128)(2,1)S(1)} %slice.135), channel_id=1, source_target_pairs={{0,2},{1,3},{2,4},{3,5},{4,6},{5,7},{6,0},{7,1},{8,10},{9,11},{10,... | collective-permute-start | bytes 786440 | tf_op jit(solution)/shard_map/ppermute | solution.py:49
  42.8 1.6 copy-start.5
  44.4 20.2 %copy-start.15 = (s32[128,4]{0,1:T(4,128)S(1)}, s32[128,4]{0,1:T(4,128)}, u32[]{:S(2)}) copy-start(s32[128,4]{0,1:T(4,128)} %param.20) | copy-start | bytes 6148
  44.4 36.7 %copy-start.16 = (s32[128]{0:T(128)S(1)}, s32[128]{0:T(128)}, u32[]{:S(2)}) copy-start(s32[128]{0:T(128)} %param.21) | copy-start | bytes 1540
  52.2 1.9 copy-start.6
  58.7 0.9 copy-start.9
  59.6 11.3 %collective-permute-start.12 = (bf16[544,384]{1,0:T(8,128)(2,1)}, bf16[544,384]{1,0:T(8,128)(2,1)S(1)}, u32[]{:S(2)}, u32[]{:S(2)}) collective-permute-start(bf16[544,384]{1,0:T(8,128)(2,1)} %get-tuple-element.76), channel_id=1, source_target_pairs={{0,16},{1,17},{2,18},{3,19},{4,20},{5,21},{6,22},{7,23},{8,24},{9,... | collective-permute-start | bytes 1253384 | tf_op jit(solution)/shard_map/ppermute | solution.py:49
  61.2 9.7 %collective-permute-start.13 = (bf16[544,384]{1,0:T(8,128)(2,1)}, bf16[544,384]{1,0:T(8,128)(2,1)S(1)}, u32[]{:S(2)}, u32[]{:S(2)}) collective-permute-start(bf16[544,384]{1,0:T(8,128)(2,1)} %get-tuple-element.77), channel_id=1, source_target_pairs={{0,48},{1,49},{2,50},{3,51},{4,52},{5,53},{6,54},{7,55},{8,56},{9,... | collective-permute-start | bytes 1253384 | tf_op jit(solution)/shard_map/ppermute | solution.py:49
  63.3 17.4 %collective-permute-start.14 = (bf16[544,384]{1,0:T(8,128)(2,1)S(1)}, bf16[544,384]{1,0:T(8,128)(2,1)S(1)}, u32[]{:S(2)}, u32[]{:S(2)}) collective-permute-start(bf16[544,384]{1,0:T(8,128)(2,1)S(1)} %get-tuple-element.78), channel_id=1, source_target_pairs={{0,32},{1,33},{2,34},{3,35},{4,36},{5,37},{6,38},{7,39},{8,40},{9,... | collective-permute-start | bytes 1253384 | tf_op jit(solution)/shard_map/ppermute | solution.py:49
  80.8 6.3 %collective-permute-start.15 = (bf16[4,2,16,256]{3,2,1,0:T(8,128)(2,1)S(1)}, bf16[4,2,16,256]{3,2,1,0:T(8,128)(2,1)S(1)}, u32[]{:S(2)}, u32[]{:S(2)}) collective-permute-start(bf16[4,2,16,256]{3,2,1,0:T(8,128)(2,1)S(1)} %pad_maximum_fusion.17), channel_id=1, source_target_pairs={{0,64},{1,65},{2,66},{3,67},{4,68},{5,69},{6,70},{7,71},{8,72},{9,... | collective-permute-start | bytes 196616 | tf_op jit(solution)/shard_map/ppermute | solution.py:49
  81.8 5.2 %copy-start.10 = (bf16[528,768]{1,0:T(8,128)(2,1)S(1)}, bf16[528,768]{1,0:T(8,128)(2,1)}, u32[]{:S(2)}) copy-start(bf16[528,768]{1,0:T(8,128)(2,1)} %copy-done.9) | copy-start | bytes 2433028
  81.9 25.6 %collective-permute-start.18 = (bf16[2048,256]{1,0:T(8,128)(2,1)S(1)}, bf16[2048,256]{1,0:T(8,128)(2,1)S(1)}, u32[]{:S(2)}, u32[]{:S(2)}) collective-permute-start(bf16[2048,256]{1,0:T(8,128)(2,1)S(1)} %pack.1.mine), channel_id=1, source_target_pairs={{0,1},{1,0},{2,3},{3,2},{4,5},{5,4},{6,7},{7,6},{8,9},{9,8},{10,11... | collective-permute-start | bytes 3145736 | tf_op jit(solution)/shard_map/ppermute | solution.py:49
  85.8 37.9 %collective-permute-start.23 = (bf16[2048,256]{1,0:T(8,128)(2,1)S(1)}, bf16[2048,256]{1,0:T(8,128)(2,1)S(1)}, u32[]{:S(2)}, u32[]{:S(2)}) collective-permute-start(bf16[2048,256]{1,0:T(8,128)(2,1)S(1)} %pack.1.mine), channel_id=1, source_target_pairs={{0,64},{1,65},{2,66},{3,67},{4,68},{5,69},{6,70},{7,71},{8,72},{9,... | collective-permute-start | bytes 3145736 | tf_op jit(solution)/shard_map/ppermute | solution.py:49
  87.1 10.0 %collective-permute-start.17 = (bf16[528,768]{1,0:T(8,128)(2,1)S(1)}, bf16[528,768]{1,0:T(8,128)(2,1)S(1)}, u32[]{:S(2)}, u32[]{:S(2)}) collective-permute-start(bf16[528,768]{1,0:T(8,128)(2,1)S(1)} %copy-done.10), channel_id=1, source_target_pairs={{0,1},{1,0},{2,3},{3,2},{4,5},{5,4},{6,7},{7,6},{8,9},{9,8},{10,11... | collective-permute-start | bytes 2433032 | tf_op jit(solution)/shard_map/ppermute | solution.py:49
  91.9 29.0 %collective-permute-start.21 = (bf16[256,1024]{1,0:T(8,128)(2,1)S(1)}, bf16[256,1024]{1,0:T(8,128)(2,1)S(1)}, u32[]{:S(2)}, u32[]{:S(2)}) collective-permute-start(bf16[256,1024]{1,0:T(8,128)(2,1)S(1)} %pad_maximum_fusion.10), channel_id=1, source_target_pairs={{0,6},{1,7},{2,0},{3,1},{4,2},{5,3},{6,4},{7,5},{8,14},{9,15},{10,... | collective-permute-start | bytes 1572872 | tf_op jit(solution)/shard_map/ppermute | solution.py:49
  94.7 2.2 %collective-permute-start.16 = (bf16[8,16,256]{2,1,0:T(8,128)(2,1)S(1)}, bf16[8,16,256]{2,1,0:T(8,128)(2,1)S(1)}, u32[]{:S(2)}, u32[]{:S(2)}) collective-permute-start(bf16[8,16,256]{2,1,0:T(8,128)(2,1)S(1)} %slice_bitcast_fusion.4), channel_id=1, source_target_pairs={{0,1},{1,0},{2,3},{3,2},{4,5},{5,4},{6,7},{7,6},{8,9},{9,8},{10,11... | collective-permute-start | bytes 196616 | tf_op jit(solution)/shard_map/ppermute | solution.py:49
  95.9 1.6 copy-start.8
  96.9 24.0 %collective-permute-start.20 = (bf16[256,1024]{1,0:T(8,128)(2,1)}, bf16[256,1024]{1,0:T(8,128)(2,1)S(1)}, u32[]{:S(2)}, u32[]{:S(2)}) collective-permute-start(bf16[256,1024]{1,0:T(8,128)(2,1)} %pad_maximum_fusion.9), channel_id=1, source_target_pairs={{0,4},{1,5},{2,6},{3,7},{4,0},{5,1},{6,2},{7,3},{8,12},{9,13},{10,... | collective-permute-start | bytes 1572872 | tf_op jit(solution)/shard_map/ppermute | solution.py:49
  97.1 26.4 %collective-permute-start.19 = (bf16[256,1024]{1,0:T(8,128)(2,1)}, bf16[256,1024]{1,0:T(8,128)(2,1)S(1)}, u32[]{:S(2)}, u32[]{:S(2)}) collective-permute-start(bf16[256,1024]{1,0:T(8,128)(2,1)} %pad_maximum_fusion.8), channel_id=1, source_target_pairs={{0,2},{1,3},{2,4},{3,5},{4,6},{5,7},{6,0},{7,1},{8,10},{9,11},{10,... | collective-permute-start | bytes 1572872 | tf_op jit(solution)/shard_map/ppermute | solution.py:49
  107.5 16.2 %collective-permute-start.22 = (f32[4,32,384]{2,1,0:T(8,128)S(1)}, f32[4,32,384]{2,1,0:T(8,128)S(1)}, u32[]{:S(2)}, u32[]{:S(2)}) collective-permute-start(f32[4,32,384]{2,1,0:T(8,128)S(1)} %slice.174), channel_id=1, source_target_pairs={{0,64},{1,65},{2,66},{3,67},{4,68},{5,69},{6,70},{7,71},{8,72},{9,... | collective-permute-start | bytes 589832 | tf_op jit(solution)/shard_map/ppermute | solution.py:49
  123.7 4.5 %collective-permute-start.24 = (bf16[2048,256]{1,0:T(8,128)(2,1)S(1)}, bf16[2048,256]{1,0:T(8,128)(2,1)S(1)}, u32[]{:S(2)}, u32[]{:S(2)}) collective-permute-start(bf16[2048,256]{1,0:T(8,128)(2,1)S(1)} %collective-permute-done.23.refs_3_.refs_1_), channel_id=1, source_target_pairs={{0,1},{1,0},{2,3},{3,2},{4,5},{5,4},{6,7},{7,6},{8,9},{9,8},{10,11... | collective-permute-start | bytes 3145736 | tf_op jit(solution)/shard_map/ppermute | solution.py:49
  124.5 13.4 %collective-permute-start.25 = (f32[2,32,384]{2,1,0:T(8,128)S(1)}, f32[2,32,384]{2,1,0:T(8,128)S(1)}, u32[]{:S(2)}, u32[]{:S(2)}) collective-permute-start(f32[2,32,384]{2,1,0:T(8,128)S(1)} %get-tuple-element.148), channel_id=1, source_target_pairs={{0,48},{1,49},{2,50},{3,51},{4,52},{5,53},{6,54},{7,55},{8,56},{9,... | collective-permute-start | bytes 294920 | tf_op jit(solution)/shard_map/ppermute | solution.py:49
  126.1 11.8 %collective-permute-start.26 = (f32[2,32,384]{2,1,0:T(8,128)S(1)}, f32[2,32,384]{2,1,0:T(8,128)S(1)}, u32[]{:S(2)}, u32[]{:S(2)}) collective-permute-start(f32[2,32,384]{2,1,0:T(8,128)S(1)} %get-tuple-element.150), channel_id=1, source_target_pairs={{0,32},{1,33},{2,34},{3,35},{4,36},{5,37},{6,38},{7,39},{8,40},{9,... | collective-permute-start | bytes 294920 | tf_op jit(solution)/shard_map/ppermute | solution.py:49
  127.2 10.7 %collective-permute-start.27 = (f32[2,32,384]{2,1,0:T(8,128)S(1)}, f32[2,32,384]{2,1,0:T(8,128)S(1)}, u32[]{:S(2)}, u32[]{:S(2)}) collective-permute-start(f32[2,32,384]{2,1,0:T(8,128)S(1)} %get-tuple-element.149), channel_id=1, source_target_pairs={{0,16},{1,17},{2,18},{3,19},{4,20},{5,21},{6,22},{7,23},{8,24},{9,... | collective-permute-start | bytes 294920 | tf_op jit(solution)/shard_map/ppermute | solution.py:49
  127.2 27.9 %collective-permute-start.36 = (bf16[1024,512]{1,0:T(8,128)(2,1)S(1)}, bf16[1024,512]{1,0:T(8,128)(2,1)S(1)}, u32[]{:S(2)}, u32[]{:S(2)}) collective-permute-start(bf16[1024,512]{1,0:T(8,128)(2,1)S(1)} %get-tuple-element.116), channel_id=1, source_target_pairs={{0,8},{1,9},{2,10},{3,11},{4,12},{5,13},{6,14},{7,15},{8,0},{9,1},... | collective-permute-start | bytes 3145736 | tf_op jit(solution)/shard_map/ppermute | solution.py:49
  138.6 8.9 %collective-permute-start.31 = (bf16[16,256]{1,0:T(8,128)(2,1)S(1)}, bf16[16,256]{1,0:T(8,128)(2,1)S(1)}, u32[]{:S(2)}, u32[]{:S(2)}) collective-permute-start(bf16[16,256]{1,0:T(8,128)(2,1)S(1)} %slice_select_fusion), channel_id=1, source_target_pairs={{0,1},{1,0},{2,3},{3,2},{4,5},{5,4},{6,7},{7,6},{8,9},{9,8},{10,11... | collective-permute-start | bytes 24584 | tf_op jit(solution)/shard_map/ppermute | solution.py:49
  139.6 8.6 %collective-permute-start.28 = (bf16[512,128]{1,0:T(8,128)(2,1)S(1)}, bf16[512,128]{1,0:T(8,128)(2,1)S(1)}, u32[]{:S(2)}, u32[]{:S(2)}) collective-permute-start(bf16[512,128]{1,0:T(8,128)(2,1)S(1)} %get-tuple-element.146), channel_id=1, source_target_pairs={{0,48},{1,49},{2,50},{3,51},{4,52},{5,53},{6,54},{7,55},{8,56},{9,... | collective-permute-start | bytes 393224 | tf_op jit(solution)/shard_map/ppermute | solution.py:49
  142.7 6.3 %collective-permute-start.29 = (bf16[512,128]{1,0:T(8,128)(2,1)S(1)}, bf16[512,128]{1,0:T(8,128)(2,1)S(1)}, u32[]{:S(2)}, u32[]{:S(2)}) collective-permute-start(bf16[512,128]{1,0:T(8,128)(2,1)S(1)} %get-tuple-element.145), channel_id=1, source_target_pairs={{0,32},{1,33},{2,34},{3,35},{4,36},{5,37},{6,38},{7,39},{8,40},{9,... | collective-permute-start | bytes 393224 | tf_op jit(solution)/shard_map/ppermute | solution.py:49
  143.3 9.1 %collective-permute-start.30 = (bf16[512,128]{1,0:T(8,128)(2,1)S(1)}, bf16[512,128]{1,0:T(8,128)(2,1)S(1)}, u32[]{:S(2)}, u32[]{:S(2)}) collective-permute-start(bf16[512,128]{1,0:T(8,128)(2,1)S(1)} %get-tuple-element.144), channel_id=1, source_target_pairs={{0,16},{1,17},{2,18},{3,19},{4,20},{5,21},{6,22},{7,23},{8,24},{9,... | collective-permute-start | bytes 393224 | tf_op jit(solution)/shard_map/ppermute | solution.py:49
  153.1 13.4 %collective-permute-start.34 = (bf16[528,512]{1,0:T(8,128)(2,1)S(1)}, bf16[528,512]{1,0:T(8,128)(2,1)S(1)}, u32[]{:S(2)}, u32[]{:S(2)}) collective-permute-start(bf16[528,512]{1,0:T(8,128)(2,1)S(1)} %head_order.1.refs_0_), channel_id=1, source_target_pairs={{0,8},{1,9},{2,10},{3,11},{4,12},{5,13},{6,14},{7,15},{8,0},{9,1},... | collective-permute-start | bytes 1622024 | tf_op jit(solution)/shard_map/ppermute | solution.py:49
  153.7 13.0 %collective-permute-start.33 = (bf16[528,512]{1,0:T(8,128)(2,1)S(1)}, bf16[528,512]{1,0:T(8,128)(2,1)S(1)}, u32[]{:S(2)}, u32[]{:S(2)}) collective-permute-start(bf16[528,512]{1,0:T(8,128)(2,1)S(1)} %head_order.1.refs_0_), channel_id=1, source_target_pairs={{0,6},{1,7},{2,0},{3,1},{4,2},{5,3},{6,4},{7,5},{8,14},{9,15},{10,... | collective-permute-start | bytes 1622024 | tf_op jit(solution)/shard_map/ppermute | solution.py:49
  154.2 14.4 %collective-permute-start.32 = (bf16[528,512]{1,0:T(8,128)(2,1)S(1)}, bf16[528,512]{1,0:T(8,128)(2,1)S(1)}, u32[]{:S(2)}, u32[]{:S(2)}) collective-permute-start(bf16[528,512]{1,0:T(8,128)(2,1)S(1)} %head_order.1.refs_0_), channel_id=1, source_target_pairs={{0,2},{1,3},{2,4},{3,5},{4,6},{5,7},{6,0},{7,1},{8,10},{9,11},{10,... | collective-permute-start | bytes 1622024 | tf_op jit(solution)/shard_map/ppermute | solution.py:49
  155.2 14.7 %collective-permute-start.37 = (bf16[1024,512]{1,0:T(8,128)(2,1)S(1)}, bf16[1024,512]{1,0:T(8,128)(2,1)S(1)}, u32[]{:S(2)}, u32[]{:S(2)}) collective-permute-start(bf16[1024,512]{1,0:T(8,128)(2,1)S(1)} %collective-permute-done.36.refs_6_.refs_5_.refs_4_), channel_id=1, source_target_pairs={{0,1},{1,0},{2,3},{3,2},{4,5},{5,4},{6,7},{7,6},{8,9},{9,8},{10,11... | collective-permute-start | bytes 3145736 | tf_op jit(solution)/shard_map/ppermute | solution.py:49
  156.5 13.3 %collective-permute-start.35 = (bf16[1024,512]{1,0:T(8,128)(2,1)S(1)}, bf16[1024,512]{1,0:T(8,128)(2,1)S(1)}, u32[]{:S(2)}, u32[]{:S(2)}) collective-permute-start(bf16[1024,512]{1,0:T(8,128)(2,1)S(1)} %get-tuple-element.115.refs_4_.refs_3_.refs_2_), channel_id=1, source_target_pairs={{0,1},{1,0},{2,3},{3,2},{4,5},{5,4},{6,7},{7,6},{8,9},{9,8},{10,11... | collective-permute-start | bytes 3145736 | tf_op jit(solution)/shard_map/ppermute | solution.py:49
  166.8 15.0 %collective-permute-start.39 = (bf16[544,512]{1,0:T(8,128)(2,1)S(1)}, bf16[544,512]{1,0:T(8,128)(2,1)S(1)}, u32[]{:S(2)}, u32[]{:S(2)}) collective-permute-start(bf16[544,512]{1,0:T(8,128)(2,1)S(1)} %pad_maximum_fusion.2), channel_id=1, source_target_pairs={{0,6},{1,7},{2,0},{3,1},{4,2},{5,3},{6,4},{7,5},{8,14},{9,15},{10,... | collective-permute-start | bytes 1671176 | tf_op jit(solution)/shard_map/ppermute | solution.py:49
  168.7 13.1 %collective-permute-start.38 = (bf16[528,512]{1,0:T(8,128)(2,1)S(1)}, bf16[528,512]{1,0:T(8,128)(2,1)S(1)}, u32[]{:S(2)}, u32[]{:S(2)}) collective-permute-start(bf16[528,512]{1,0:T(8,128)(2,1)S(1)} %pad_maximum_fusion.5), channel_id=1, source_target_pairs={{0,2},{1,3},{2,4},{3,5},{4,6},{5,7},{6,0},{7,1},{8,10},{9,11},{10,... | collective-permute-start | bytes 1622024 | tf_op jit(solution)/shard_map/ppermute | solution.py:49
  168.8 11.6 %collective-permute-start.40 = (bf16[512,512]{1,0:T(8,128)(2,1)S(1)}, bf16[512,512]{1,0:T(8,128)(2,1)S(1)}, u32[]{:S(2)}, u32[]{:S(2)}) collective-permute-start(bf16[512,512]{1,0:T(8,128)(2,1)S(1)} %pad_maximum_fusion.11), channel_id=1, source_target_pairs={{0,8},{1,9},{2,10},{3,11},{4,12},{5,13},{6,14},{7,15},{8,0},{9,1},... | collective-permute-start | bytes 1572872 | tf_op jit(solution)/shard_map/ppermute | solution.py:49
  181.8 7.6 %collective-permute-start.42 = (bf16[272,512]{1,0:T(8,128)(2,1)S(1)}, bf16[272,512]{1,0:T(8,128)(2,1)S(1)}, u32[]{:S(2)}, u32[]{:S(2)}) collective-permute-start(bf16[272,512]{1,0:T(8,128)(2,1)S(1)} %slice.163), channel_id=1, source_target_pairs={{0,6},{1,7},{2,0},{3,1},{4,2},{5,3},{6,4},{7,5},{8,14},{9,15},{10,... | collective-permute-start | bytes 835592 | tf_op jit(solution)/shard_map/ppermute | solution.py:49
  182.9 6.5 %collective-permute-start.41 = (bf16[256,512]{1,0:T(8,128)(2,1)S(1)}, bf16[256,512]{1,0:T(8,128)(2,1)S(1)}, u32[]{:S(2)}, u32[]{:S(2)}) collective-permute-start(bf16[256,512]{1,0:T(8,128)(2,1)S(1)} %slice.162), channel_id=1, source_target_pairs={{0,2},{1,3},{2,4},{3,5},{4,6},{5,7},{6,0},{7,1},{8,10},{9,11},{10,... | collective-permute-start | bytes 786440 | tf_op jit(solution)/shard_map/ppermute | solution.py:49
  190.4 6.2 %collective-permute-start.43 = (f32[528,256]{1,0:T(8,128)S(1)}, f32[528,256]{1,0:T(8,128)S(1)}, u32[]{:S(2)}, u32[]{:S(2)}) collective-permute-start(f32[528,256]{1,0:T(8,128)S(1)} %get-tuple-element.127), channel_id=1, source_target_pairs={{0,1},{1,0},{2,3},{3,2},{4,5},{5,4},{6,7},{7,6},{8,9},{9,8},{10,11... | collective-permute-start | bytes 1622024 | tf_op jit(solution)/shard_map/ppermute | solution.py:49
